TPU v7x, 128 devices: a whole 4x4x4 slice. The times are simulated.
128 devices in a mesh: ctx: 16 (over y, z_hi, core), fsdp: 8 (over z_lo, x).
Axes of the slice: x: 4, y: 4, z: 4 (z_hi: 2, z_lo: 2; z = z_hi * 2 + z_lo), core: 2. Of those that a mesh axis runs over, the one named last changes fastest.
Arguments:
- decoder_in: bfloat16 [8, 2048, 768], P('fsdp', 'ctx'), may hold values from -6 to 6
- encoder_states: bfloat16 [8, 1024, 768], P('fsdp', 'ctx'), may hold values from -6 to 6
- out_grad: bfloat16 [8, 2048, 768], P('fsdp', 'ctx'), may hold values from -6 to 6
- block_pairs: int32 [16], replicated, may hold values from 0 to 15, each once
- bucket_table: int32 [128], replicated, may hold values from 0 to 31, as said below
- gain_self: bfloat16 [768], P('fsdp'), may hold values from 0.25 to 1.75
- self_query: bfloat16 [768, 768], P('fsdp'), may hold values from -0.078125 to 0.078125
- self_key: bfloat16 [768, 768], P('fsdp'), may hold values from -0.078125 to 0.078125
- self_value: bfloat16 [768, 768], P('fsdp'), may hold values from -0.21875 to 0.21875
- self_out: bfloat16 [768, 768], P('fsdp'), may hold values from -2.5 to 2.5
- position_bias: bfloat16 [32, 12], P('fsdp'), may hold values from -4 to 4
- gain_cross: bfloat16 [768], P('fsdp'), may hold values from 0.25 to 1.75
- cross_query: bfloat16 [768, 768], P('fsdp'), may hold values from -0.078125 to 0.078125
- cross_key: bfloat16 [768, 768], P('fsdp'), may hold values from -0.078125 to 0.078125
- cross_value: bfloat16 [768, 768], P('fsdp'), may hold values from -0.21875 to 0.21875
- cross_out: bfloat16 [768, 768], P('fsdp'), may hold values from -3.5 to 3.5
- gain_feed: bfloat16 [768], P('fsdp'), may hold values from 0.25 to 1.75
- feed_gate: bfloat16 [768, 2048], P('fsdp'), may hold values from -0.21875 to 0.21875
- feed_up: bfloat16 [768, 2048], P('fsdp'), may hold values from -0.21875 to 0.21875
- feed_down: bfloat16 [2048, 768], P('fsdp'), may hold values from -0.125 to 0.125
Outputs:
- block_out: float32 [8, 2048, 768], P('fsdp', 'ctx')
- grad_decoder: float32 [8, 2048, 768], P('fsdp', 'ctx')
- grad_encoder: float32 [8, 1024, 768], P('fsdp', 'ctx')
- grad_gain_self: float32 [768], P('fsdp')
- grad_self_query: float32 [768, 768], P('fsdp')
- grad_self_key: float32 [768, 768], P('fsdp')
- grad_self_value: float32 [768, 768], P('fsdp')
- grad_self_out: float32 [768, 768], P('fsdp')
- grad_position_bias: float32 [32, 12], P('fsdp')
- grad_gain_cross: float32 [768], P('fsdp')
- grad_cross_query: float32 [768, 768], P('fsdp')
- grad_cross_key: float32 [768, 768], P('fsdp')
- grad_cross_value: float32 [768, 768], P('fsdp')
- grad_cross_out: float32 [768, 768], P('fsdp')
- grad_gain_feed: float32 [768], P('fsdp')
- grad_feed_gate: float32 [768, 2048], P('fsdp')
- grad_feed_up: float32 [768, 2048], P('fsdp')
- grad_feed_down: float32 [2048, 768], P('fsdp')
Inputs may be any that keep to these rules, and one draw needn't show every extreme that they name: block_pairs is a permutation of 0 to 15. `bucket_table`: entry n is the bucket of distance n (distances of 127 and more use the last entry); it never falls along n, is 0 at n = 0 and 31 at n = 127.
All inputs are finite; a program needn't handle non-finite values.
Results may differ from a plain program's by a relative error of at most 0.03.
Values may be sent and summed in bfloat16 or wider, within the bound.
A program may use at most 192 MiB of HBM per device.

v0:
```python
import functools

import jax
import jax.numpy as jnp
from jax import lax
from jax.experimental import pallas as pl
from jax.experimental.pallas import tpu as pltpu
from jax.sharding import PartitionSpec as P

D = 768
FF = 2048
HEADS = 12
HEAD_DIM = 64
PAIRS = HEADS // 2
N_CTX = 16
TOK = 128
ENC = 64
HALF = 64
REACH = 128
BF = jnp.bfloat16
F32 = jnp.float32
MIB = 1024 * 1024


def ctx_place():
    me = lax.axis_index("ctx")
    core = me % 2
    high = (me // 2) % 2
    y = me // 4
    return me, core, high, y


def slot_of(y, shift, high, core):
    return ((y + shift) % 4) * 4 + 2 * high + core


def split_heads(block):
    lane = lax.broadcasted_iota(jnp.int32, block.shape, 1)
    nothing = jnp.zeros_like(block)
    return jnp.concatenate(
        [jnp.where(lane < HEAD_DIM, block, nothing), jnp.where(lane < HEAD_DIM, nothing, block)],
        axis=0,
    )


def join_heads(transposed):
    row = lax.broadcasted_iota(jnp.int32, (2 * HEAD_DIM, TOK), 0)
    return jnp.where(row < HEAD_DIM, transposed[:, :TOK], transposed[:, TOK:]).T


def contract(left, right, dims):
    return lax.dot_general(left, right, (dims, ((), ())), preferred_element_type=F32)


def key_chunk(ref, j):
    if ref.shape[2] == 2 * HALF:
        return ref[j, 0]
    return ref[pl.ds(2 * j, 2), 0].reshape(2 * HALF, 2 * HEAD_DIM)


def bias_chunk(class_ref, tile_ref, j, first=0):
    lane = lax.broadcasted_iota(jnp.int32, (HALF, TOK), 1)
    rows = []
    for half in range(2):
        spot = 2 * j + half
        near = class_ref[0, spot]
        far = class_ref[1, spot]
        rows.append(
            jnp.concatenate(
                [
                    jnp.where(lane < HALF, tile_ref[first + head, near], tile_ref[first + head, far])
                    for head in range(2)
                ],
                axis=1,
            )
        )
    return jnp.concatenate(rows, axis=0)


def fold(values, join):
    return join(values.reshape(-1, 8, values.shape[-1]), axis=0)


def attend_pair(queries, keys, values, bias, score_ref, share_ref, chunks):
    queries = split_heads(queries)
    highest = None
    for j in range(chunks):
        scores = contract(keys(j), queries, ((1,), (1,)))
        if bias is not None:
            scores = scores + bias(j)
        score_ref[j] = scores
        top = fold(scores, jnp.max)
        highest = top if highest is None else jnp.maximum(highest, top)
    highest = jnp.max(highest, axis=0, keepdims=True)
    summed = jnp.zeros((8, 2 * TOK), F32)
    for j in range(chunks):
        raised = jnp.exp(score_ref[j] - highest)
        summed = summed + fold(raised, jnp.sum)
        share_ref[j] = raised.astype(BF)
    summed = jnp.sum(summed, axis=0, keepdims=True)
    gathered = jnp.concatenate([values(j) for j in range(chunks)], axis=0)
    mixed = contract(gathered, share_ref[:chunks].reshape(-1, 2 * TOK), ((0,), (0,)))
    return join_heads(mixed / summed).astype(BF), highest + jnp.log(summed)


def attend_pairs(first, last, kv_ref, query_ref, out_ref, total_ref, score_ref, share_ref, bias=None):
    rows = kv_ref.shape[2]
    chunks = N_CTX * rows // TOK

    def step(pair, carry):
        cut = pl.ds(pl.multiple_of(pair * TOK, TOK), TOK)

        def chunk(part, j):
            if rows == TOK:
                return kv_ref[j, part, :, cut]
            return kv_ref[2 * j : 2 * j + 2, part, :, cut].reshape(TOK, TOK)

        mixed, total = attend_pair(
            query_ref[:, cut],
            functools.partial(chunk, 0),
            functools.partial(chunk, 1),
            None if bias is None else functools.partial(bias, pair),
            score_ref,
            share_ref,
            chunks,
        )
        out_ref[:, cut] = mixed
        total_ref[pair] = jnp.broadcast_to(total, (8, 2 * TOK))
        return carry

    lax.fori_loop(first, last, step, 0)


def strip_hot():
    shape = (REACH, 3 * TOK)
    spot = lax.broadcasted_iota(jnp.int32, shape, 1)
    distance = jnp.clip(HALF * (spot // TOK) + spot % TOK - (HALF - 1), 0, REACH - 1)
    return (distance == lax.broadcasted_iota(jnp.int32, shape, 0)).astype(BF)


def index_tables(me, pairs_ref, class_ref, near_ref):
    own = pairs_ref[me]
    for half in range(2):
        query = 31 - own if half else own
        spots = [jnp.int32(-1)] * 3
        for block in range(32):
            pair = pairs_ref[block // 2]
            key = 31 - pair if block % 2 else pair
            gap = query - key
            class_ref[half, block] = jnp.where(gap < 0, 4, jnp.minimum(gap, 3))
            for near in range(3):
                spots[near] = jnp.where(gap == near, block, spots[near])
        for near in range(3):
            near_ref[half, near] = spots[near]


def build_tiles(bias_rows, strips, tile_ref):
    lane = lax.broadcasted_iota(jnp.int32, (HALF, TOK), 1)
    key = lax.broadcasted_iota(jnp.int32, (HALF, TOK), 0)
    row = jnp.where(lane < HALF, lane, lane - HALF)
    for head in range(HEADS):
        for gap in range(3):
            strip = strips[head : head + 1, gap * TOK : gap * TOK + TOK]
            turned = pltpu.roll(
                jnp.broadcast_to(strip, (HALF, TOK)), 65, 1, stride=1, stride_axis=0
            )
            tile = jnp.where(lane < HALF, turned, pltpu.roll(turned, HALF, 1))
            if gap == 0:
                tile = jnp.where(key > row, -1e30, tile)
            tile_ref[head, gap] = tile
        tile_ref[head, 3] = jnp.broadcast_to(bias_rows[head : head + 1, REACH - 1 :], (HALF, TOK))
        tile_ref[head, 4] = jnp.full((HALF, TOK), -1e30, F32)


def torus_place():
    me, core, high, y = ctx_place()
    shard = lax.axis_index("fsdp")
    return me, core, high, y, shard // 4, shard % 4


def hop(src, dst, send_sem, recv_sem, ctx, fsdp):
    return pltpu.make_async_remote_copy(
        src_ref=src,
        dst_ref=dst,
        send_sem=send_sem,
        recv_sem=recv_sem,
        device_id={"ctx": ctx, "fsdp": fsdp},
    )


def greet_all(devices):
    barrier = pltpu.get_barrier_semaphore()
    for ctx, fsdp in devices:
        pl.semaphore_signal(barrier, inc=1, device_id={"ctx": ctx, "fsdp": fsdp})
    pl.semaphore_wait(barrier, len(devices))


ROOT = (2.0 / 3.141592653589793) ** 0.5
PACKS = ((0, 1), (2, 3), (4, 5, 6, 7), (8, 9), (10,))


def front_kernel(*refs):
    sources = refs[:11]
    small_ref, token_ref, state_ref, upstream_ref, bucket_ref, pairs_ref = refs[11:17]
    results = refs[17:20]
    (
        gain_out, normed_out, query_out, tile_ref, attended_ref, total_ref, mid_one_ref,
        normed_two_ref, cross_query_ref, cross_attended_ref, cross_total_ref,
        block_ref, d_mid_ref, branch_ref, d_cross_ref, gain_grad_ref,
        wide_mine, wide_inner, wide_outer, tall_mine, tall_inner, tall_outer,
        class_ref, near_ref, self_result, cross_result,
    ) = refs[20:46]
    targets = refs[46:51]
    (
        self_out_ref, cross_out_ref, landing, self_ref, cross_ref, score_ref, share_ref,
        feed_left, feed_right, slope_ref, turned, turned_hidden,
        send_sem, x_sem, z_sem, core_sem,
        fill_sem, small_sem, self_sem, cross_sem, feed_sem, local_sem,
    ) = refs[51:]
    me, core, high, y, low, x = torus_place()
    shard = low * 4 + x
    sibling = (slot_of(y, 0, high, 1 - core), shard)
    inside = (me, (1 - low) * 4 + x)
    outside = (slot_of(y, 0, 1 - high, core), (1 - low) * 4 + x)
    across = slot_of(y, 0, 1 - high, core)
    ahead, behind = (slot_of(y, shift, high, core) for shift in (1, 3))
    others = [low * 4 + (x + shift) % 4 for shift in (1, 2, 3)]
    peers = [(shard + shift) % 8 for shift in range(1, 8)]
    greet_all(
        [sibling, outside, (across, shard), (ahead, shard), (behind, shard)]
        + [(me, peer) for peer in peers]
    )
    sends = []

    def send(src, dst, recv_sem, device):
        copy = hop(src, dst, send_sem.at[len(sends)], recv_sem, *device)
        copy.start()
        sends.append(copy)

    def arrived(ref, recv_sem):
        hop(ref, ref, send_sem.at[0], recv_sem, *sibling).wait_recv()

    def bring(src, dst, sem):
        copy = pltpu.make_async_copy(src, dst, sem)
        copy.start()
        return copy


    def part(k, owner, whose, side=None):
        ref = targets[k]
        count = ref.shape[1] // 2
        start = pl.multiple_of(whose * count, 16)
        if side is None:
            return ref.at[owner, pl.ds(start, count), :]
        width = ref.shape[2] // 2
        return ref.at[owner, pl.ds(start, count), pl.ds(side * width, width)]

    def fill(k):
        copies = []
        start = 0
        for source in PACKS[k]:
            width = sources[source].shape[1]
            copies.append(
                bring(
                    sources[source],
                    targets[k].at[shard, :, pl.ds(start, width)],
                    fill_sem.at[source],
                )
            )
            start += width
        return copies

    def send_own(k):
        for copy in fills[k]:
            copy.wait()
        for spot in (1, 0, 2):
            block = part(k, shard, core)
            send(block, block, x_sem.at[k, spot], (me, others[spot]))
        for side, device in enumerate((inside, outside)):
            piece = part(k, shard, core, side)
            send(piece, piece, z_sem.at[k, 3, side], device)


    def pass_x(k):
        for spot in (0, 2, 1):
            owner = low * 4 + (x + 3 - spot) % 4
            block = part(k, owner, core)
            arrived(block, x_sem.at[k, spot])
            for side, device in enumerate((inside, outside)):
                piece = part(k, owner, core, side)
                send(piece, piece, z_sem.at[k, spot, side], device)
            send(block, block, core_sem.at[k, spot], sibling)

    def pass_z(k):
        for spot in (3, 0, 2, 1):
            owner = (1 - low) * 4 + (x + 3 - spot) % 4
            for side in range(2):
                piece = part(k, owner, core, side)
                arrived(piece, z_sem.at[k, spot, side])
                send(piece, piece, core_sem.at[k, 3 + 2 * spot + side], sibling)

    def complete(k):
        for spot in range(3):
            owner = low * 4 + (x + 3 - spot) % 4
            arrived(part(k, owner, 1 - core), core_sem.at[k, spot])
        for spot in range(4):
            owner = (1 - low) * 4 + (x + 3 - spot) % 4
            for side in range(2):
                arrived(part(k, owner, 1 - core, side), core_sem.at[k, 3 + 2 * spot + side])


    def kv_start(src, out, sems):
        send(src, out.at[me], sems.at[me, 0], (across, shard))
        send(src, out.at[me], sems.at[me, 0], (ahead, shard))
        send(src, out.at[me], sems.at[me, 0], (behind, shard))
        send(src, out.at[me], sems.at[me, 0], sibling)

    def kv_across(out, sems):
        block = out.at[across]
        arrived(block, sems.at[across, 0])
        send(block, block, sems.at[across, 0], (ahead, shard))
        send(block, block, sems.at[across, 0], (behind, shard))
        send(block, block, sems.at[across, 0], sibling)

    def kv_near(out, sems, flip):
        half = 1 - high if flip else high
        slot = slot_of(y, 1, half, core)
        block = out.at[slot]
        arrived(block, sems.at[slot, 0])
        send(block.at[0], block.at[0], sems.at[slot, 0], (behind, shard))
        send(block, block, sems.at[slot, 0], sibling)
        slot = slot_of(y, 3, half, core)
        block = out.at[slot]
        arrived(block, sems.at[slot, 0])
        send(block.at[1], block.at[1], sems.at[slot, 1], (ahead, shard))
        send(block, block, sems.at[slot, 0], sibling)

    def kv_far(out, sems, flip):
        slot = slot_of(y, 2, 1 - high if flip else high, core)
        for part in range(2):
            arrived(out.at[slot, part], sems.at[slot, part])
        send(out.at[slot], out.at[slot], sems.at[slot, 0], sibling)

    def kv_complete(out, sems):
        for shift in range(4):
            for half in range(2):
                slot = slot_of(y, shift, half, 1 - core)
                arrived(out.at[slot], sems.at[slot, 0])

    fills = [fill(k) for k in range(5)]
    own_small = bring(small_ref, landing.at[shard], local_sem.at[0])
    for spot, peer in enumerate(peers):
        send(small_ref, landing.at[shard], small_sem.at[spot], (me, peer))
    send_own(0)
    send_own(1)
    own_small.wait()
    for spot in range(7):
        arrived(landing.at[(shard + 7 - spot) % 8], small_sem.at[spot])
    gains = landing[...].astype(F32)
    gain = [
        jnp.concatenate([gains[owner, k : k + 1, :96] for owner in range(8)], axis=1)
        for k in range(3)
    ]
    for k in range(3):
        gain_out[k : k + 1, :] = gain[k]
    tokens = token_ref[...].astype(F32)
    normed = rms_scaled(tokens, gain[0])
    normed_out[...] = normed
    pass_x(0)
    send_own(2)
    pass_z(0)
    pass_x(1)
    send_own(3)
    complete(0)
    exits = [bring(targets[0], results[0], local_sem.at[1])]
    for half in range(2):
        weight = targets[0][:, :, half * D : half * D + D].reshape(D, D)
        self_ref[half] = matmul(normed, weight).astype(BF)
    kv_start(self_ref, self_out_ref, self_sem)
    own_self = bring(self_ref, self_out_ref.at[me], local_sem.at[2])
    pass_z(1)
    complete(1)
    exits.append(bring(targets[1], results[1], local_sem.at[4]))
    for half in range(2):
        weight = targets[1][:, :, half * D : half * D + D].reshape(D, D)
        cross_ref[half] = matmul(state_ref[...], weight).astype(BF)
    kv_start(cross_ref, cross_out_ref, cross_sem)
    own_cross = bring(cross_ref, cross_out_ref.at[me], local_sem.at[3])
    index_tables(me, pairs_ref, class_ref, near_ref)
    slab = lax.broadcasted_iota(jnp.int32, (128, REACH), 0)
    place = slab % 16 - 3
    wanted = jnp.where((place >= 0) & (place < 4), 4 * (slab // 16) + place, -1)
    hot = jnp.where(wanted == bucket_ref[...], 1.0, 0.0).astype(BF)
    bias_rows = contract(landing[...].reshape(128, 128), hot, ((0,), (0,)))[:16]
    build_tiles(bias_rows, matmul(bias_rows.astype(BF), strip_hot()), tile_ref)
    kv_across(self_out_ref, self_sem)
    pass_x(2)
    send_own(4)
    kv_near(self_out_ref, self_sem, False)
    pass_z(2)
    kv_across(cross_out_ref, cross_sem)
    kv_near(self_out_ref, self_sem, True)
    pass_x(3)
    complete(2)
    exits.append(bring(targets[2], results[2], local_sem.at[5]))

    def square(k):
        return targets[2][:, :, k * D : k * D + D].reshape(D, D)

    query_out[...] = matmul(normed, square(0)).astype(BF)
    kv_far(self_out_ref, self_sem, False)
    kv_far(self_out_ref, self_sem, True)
    kv_near(cross_out_ref, cross_sem, False)
    own_self.wait()
    own_cross.wait()
    kv_complete(self_out_ref, self_sem)
    exits.append(bring(self_out_ref, self_result, local_sem.at[6]))

    def attend_self(first, last):
        attend_pairs(
            first, last, self_out_ref, query_out, attended_ref, total_ref, score_ref, share_ref,
            lambda pair, j: bias_chunk(class_ref, tile_ref, j, 2 * pair),
        )

    def attend_cross(first, last):
        attend_pairs(
            first, last, cross_out_ref, cross_query_ref, cross_attended_ref, cross_total_ref,
            score_ref, share_ref,
        )

    attend_self(0, 2)
    pass_x(4)
    kv_near(cross_out_ref, cross_sem, True)
    kv_far(cross_out_ref, cross_sem, False)
    attend_self(2, 4)
    pass_z(3)
    kv_far(cross_out_ref, cross_sem, True)
    attend_self(4, 6)
    mid_one = tokens + matmul(attended_ref[...], square(1))
    mid_one_ref[...] = mid_one
    normed_two = rms_scaled(mid_one, gain[1])
    normed_two_ref[...] = normed_two
    cross_query_ref[...] = matmul(normed_two, square(2)).astype(BF)
    pass_z(4)
    kv_complete(cross_out_ref, cross_sem)
    exits.append(bring(cross_out_ref, cross_result, local_sem.at[7]))
    attend_cross(0, 3)
    complete(3)
    attend_cross(3, 6)
    complete(4)
    mid_two = mid_one_ref[...] + matmul(cross_attended_ref[...], square(3))


    normed_three = rms_scaled(mid_two, gain[2])
    upstream = upstream_ref[...]
    near_rows, far_rows = pl.ds(0, TOK), pl.ds(TOK, TOK)
    feed_left[near_rows, :D] = normed_three
    for piece in range(4):
        start = piece * 512
        gate = matmul(normed_three, targets[3][:, :, start : start + 512].reshape(D, 512))
        up = matmul(normed_three, targets[3][:, :, FF + start : FF + start + 512].reshape(D, 512))
        gate = gate.astype(BF).astype(F32)
        up = up.astype(BF).astype(F32)
        square_gate = gate * gate
        curve = jnp.tanh(ROOT * (gate + 0.044715 * gate * square_gate))
        raised = 0.5 * gate * (1.0 + curve)
        steep = 0.5 * (1.0 + curve) + 0.5 * gate * (1.0 - curve * curve) * (
            ROOT * (1.0 + 3.0 * 0.044715 * square_gate)
        )
        d_hidden = contract(
            upstream, targets[4][2 * piece : 2 * piece + 2].reshape(512, D), ((1,), (1,))
        )
        feed_left[near_rows, D + start : D + start + 512] = (raised * up).astype(BF)
        slope_ref[0, :, start : start + 512] = (d_hidden * up * steep).astype(BF)
        slope_ref[1, :, start : start + 512] = (d_hidden * raised).astype(BF)
    half = D // 2
    near_half = pl.ds(pl.multiple_of(core * half, 128), half)
    far_half = pl.ds(pl.multiple_of((1 - core) * half, 128), half)
    swaps = []
    for index, (src, dst) in enumerate(
        (
            (feed_left.at[near_rows], feed_left.at[far_rows]),
            (slope_ref.at[1 - core], feed_right.at[far_rows, pl.ds(0, FF)]),
            (upstream_ref.at[:, far_half], feed_right.at[far_rows, pl.ds(FF, half)]),
        )
    ):
        copy = hop(src, dst, feed_sem.at[0, index], feed_sem.at[1, index], *sibling)
        copy.start()
        swaps.append(copy)
    feed_right[near_rows, :FF] = slope_ref[core]
    feed_right[near_rows, FF:] = upstream_ref[:, near_half]
    block_ref[...] = mid_two + matmul(feed_left[near_rows, D:], targets[4][...].reshape(FF, D))
    grad = contract(slope_ref[0], targets[3][:, :, :FF].reshape(D, FF), ((1,), (1,)))
    grad = grad + contract(slope_ref[1], targets[3][:, :, FF:].reshape(D, FF), ((1,), (1,)))
    inverse = lax.rsqrt(jnp.mean(mid_two * mid_two, axis=-1, keepdims=True) + 1e-06)
    gain_grad_ref[...] = jnp.sum(mid_two * inverse * grad, axis=0, keepdims=True)
    scaled = gain[2] * grad
    mixed = jnp.mean(mid_two * scaled, axis=-1, keepdims=True)
    d_mid_two = upstream.astype(F32) + (
        inverse * scaled - mid_two * (inverse * inverse * inverse * mixed)
    )
    d_mid_ref[...] = d_mid_two
    branch_ref[...] = d_mid_two.astype(BF)
    d_cross_ref[...] = contract(d_mid_two.astype(BF), square(3), ((1,), (1,))).astype(BF)
    for copy in swaps:
        copy.wait_recv()
    turned[...] = feed_left[:, :D].T.reshape(8, 96, 2 * TOK)
    turned_hidden[...] = feed_left[:, D:].T.reshape(8, FF // 8, 2 * TOK)
    for group in range(2):
        owners = pl.ds(4 * ((1 - low + group) % 2), 4)
        left = turned[owners].reshape(4 * 96, 2 * TOK)
        for piece in range(4):
            cut = slice(piece * 512, piece * 512 + 512)
            part = matmul(left, feed_right[:, cut]).astype(BF).reshape(4, 96, 512)
            if group:
                wide_mine[:, :, cut] = part
            else:
                wide_inner[:, :, cut] = part[:, :48]
                wide_outer[:, :, cut] = part[:, 48:]
        left = turned_hidden[owners].reshape(4 * FF // 8, 2 * TOK)
        part = matmul(left, feed_right[:, FF:]).astype(BF).reshape(4, FF // 8, half)
        if group:
            tall_mine[...] = part
        else:
            tall_inner[...] = part[:, :128]
            tall_outer[...] = part[:, 128:]
    for copy in sends + swaps:
        copy.wait_send()
    for copy in exits:
        copy.wait()


def front(weights, others, collective_id):
    dma = pltpu.SemaphoreType.DMA
    packs = [
        (8, weights[group[0]].shape[0], sum(weights[k].shape[1] for k in group)) for group in PACKS
    ]
    anywhere = pl.BlockSpec(memory_space=pl.ANY)
    inside = pl.BlockSpec(memory_space=pltpu.VMEM)
    scalars = pl.BlockSpec(memory_space=pltpu.SMEM)
    return pl.pallas_call(
        front_kernel,
        out_shape=[jax.ShapeDtypeStruct(pack, BF) for pack in packs[:3]]
        + [
            jax.ShapeDtypeStruct((3, D), F32),
            jax.ShapeDtypeStruct((TOK, D), BF),
            jax.ShapeDtypeStruct((TOK, D), BF),
            jax.ShapeDtypeStruct((HEADS, 5, HALF, TOK), F32),
            jax.ShapeDtypeStruct((TOK, D), BF),
            jax.ShapeDtypeStruct((PAIRS, 8, 2 * TOK), F32),
            jax.ShapeDtypeStruct((TOK, D), F32),
            jax.ShapeDtypeStruct((TOK, D), BF),
            jax.ShapeDtypeStruct((TOK, D), BF),
            jax.ShapeDtypeStruct((TOK, D), BF),
            jax.ShapeDtypeStruct((PAIRS, 8, 2 * TOK), F32),
            jax.ShapeDtypeStruct((TOK, D), F32),
            jax.ShapeDtypeStruct((TOK, D), F32),
            jax.ShapeDtypeStruct((TOK, D), BF),
            jax.ShapeDtypeStruct((TOK, D), BF),
            jax.ShapeDtypeStruct((1, D), F32),
            jax.ShapeDtypeStruct((4, 96, FF), BF),
            jax.ShapeDtypeStruct((4, 48, FF), BF),
            jax.ShapeDtypeStruct((4, 48, FF), BF),
            jax.ShapeDtypeStruct((4, 256, D // 2), BF),
            jax.ShapeDtypeStruct((4, 128, D // 2), BF),
            jax.ShapeDtypeStruct((4, 128, D // 2), BF),
            jax.ShapeDtypeStruct((2, 32), jnp.int32),
            jax.ShapeDtypeStruct((2, 3), jnp.int32),
            jax.ShapeDtypeStruct((N_CTX, 2, TOK, D), BF),
            jax.ShapeDtypeStruct((N_CTX, 2, ENC, D), BF),
        ],
        in_specs=[anywhere] * 12 + [inside] * 4 + [scalars],
        out_specs=[anywhere] * 3 + [inside] * 22 + [scalars] * 2 + [anywhere] * 2,
        scratch_shapes=[pltpu.VMEM(pack, BF) for pack in packs]
        + [
            pltpu.VMEM((N_CTX, 2, TOK, D), BF),
            pltpu.VMEM((N_CTX, 2, ENC, D), BF),
            pltpu.VMEM((8, 16, 128), BF),
            pltpu.VMEM((2, TOK, D), BF),
            pltpu.VMEM((2, ENC, D), BF),
            pltpu.VMEM((N_CTX, TOK, 2 * TOK), F32),
            pltpu.VMEM((N_CTX, TOK, 2 * TOK), BF),
            pltpu.VMEM((2 * TOK, D + FF), BF),
            pltpu.VMEM((2 * TOK, FF + D // 2), BF),
            pltpu.VMEM((2, TOK, FF), BF),
            pltpu.VMEM((8, 96, 2 * TOK), BF),
            pltpu.VMEM((8, FF // 8, 2 * TOK), BF),
            dma((5 * 22 + 7 + 2 * 18,)),
            dma((5, 3)),
            dma((5, 4, 2)),
            dma((5, 11)),
            dma((11,)),
            dma((7,)),
            dma((N_CTX, 2)),
            dma((N_CTX, 2)),
            dma((2, 3)),
            dma((8,)),
        ],
        compiler_params=pltpu.CompilerParams(
            collective_id=collective_id, has_side_effects=True, vmem_limit_bytes=60 * MIB
        ),
        name="front",
    )(*weights, *others)


PIECE = 96
WIDTHS = (D // 2, D // 2, D // 2, D // 2, D, D, FF)
SPAN = sum(WIDTHS)
DOWN = len(WIDTHS)
CHUNKS = DOWN + 1
CROSS_KV, SELF_KV, WIDE = 4, 5, 6
LEFT = (D,) * 4
RIGHT = (D // 2,) * 4


def finish_kernel(*refs):
    lefts = refs[:4]
    rights = refs[4:8]
    wide_refs, down_refs = refs[8:11], refs[11:14]
    dkv_ref, dckv_ref, square_ref = refs[14:17]
    state_ref, kv_ref, ckv_ref, dq_ref, dmid_ref, token_ref, gain_ref, small_ref = refs[17:25]
    early_out, late_out, small_out, decoder_ref, encoder_ref = refs[25:30]
    (
        left_all, right_all, turned, turned_one, turned_state, state_all, s_right, c_right,
        kept, from_z, from_x, via_x, d_z, d_x, d_via,
        s_kept, s_core, s_row, s_via, s_stage, s_high, s_fin,
        c_kept, c_core, c_row, c_via, c_stage, c_high, c_fin,
        small_f32, sm_own, sm_core, sm_z, sm_x, sm_ctx, sm_total,
        packed, from_ctx, land, late_packed, late_from, late_land,
        wide_add, down_add, query_ref, bring_sem,
        s_sem, c_sem, fill_sem, act_send, act_recv, late_send, late_recv, z_send, z_recv,
        x_send, x_recv, ctx_send, ctx_recv, pass_send, pass_recv, sm_send, sm_recv, local_sem,
    ) = refs[30:]
    me, core, high, y, low, x = torus_place()
    shard = low * 4 + x
    rank = y * 2 + high
    sibling = (slot_of(y, 0, high, 1 - core), shard)
    inside = (me, (1 - low) * 4 + x)
    outside = (slot_of(y, 0, 1 - high, core), (1 - low) * 4 + x)
    across = (slot_of(y, 0, 1 - high, core), shard)
    others = [low * 4 + (x + shift) % 4 for shift in (1, 2, 3)]
    ahead = (slot_of(y, 1, high, core), shard)
    behind = (slot_of(y, 3, high, core), shard)
    shifts = [(dy, dz) for dy in range(4) for dz in range(2)][1:]
    mates = [((y + dy) % 4) * 2 + (high + dz) % 2 for dy, dz in shifts]
    greet_all(
        [sibling, inside, outside]
        + [(me, other) for other in others]
        + [(mate * 2 + core, shard) for mate in mates]
    )
    sends = []

    def go(src, dst, send_sem, recv_sem, device):
        copy = hop(src, dst, send_sem, recv_sem, *device)
        copy.start()
        sends.append(copy)
        return copy

    def bring(src, dst, sem):
        copy = pltpu.make_async_copy(src, dst, sem)
        copy.start()
        return copy


    def rows_start(source, held, arrived, sem):
        over = []
        local = []
        for spot, shift in enumerate((2, 1, 3, 0)):
            pair = pl.ds(((y + shift) % 4) * 2, 2)
            block = pl.ds(2 * spot, 2)
            over.append(
                go(
                    source.at[pair, 1 - core], arrived.at[block],
                    sem.at[0, spot], sem.at[1, spot], sibling,
                )
            )
            local.append(bring(source.at[pair, core], held.at[block], sem.at[4, spot]))
        return over, local


    def rows_send(copies, held, arrived, via, row, sem):
        over, local = copies
        onward = []
        for spot in range(4):
            local[spot].wait()
            over[spot].wait_recv()
            for block in (2 * spot, 2 * spot + 1):
                for part in range(2):
                    held[block, part] = held[block, part] + arrived[block, part]
            if spot == 0:
                first = go(held.at[0], via.at[0], sem.at[2, 0], sem.at[3, 0], ahead)
                second = go(held.at[1], via.at[1], sem.at[2, 1], sem.at[3, 1], behind)
            elif spot == 1:
                onward.append(go(held.at[3], row.at[0, 1], sem.at[2, 2], sem.at[3, 2], ahead))
            elif spot == 2:
                onward.append(go(held.at[4], row.at[1, 0], sem.at[2, 3], sem.at[3, 3], behind))
        return first, second, onward

    def rows_via(state, held, via, row, sem):
        first, second, onward = state
        first.wait_recv()
        for part in range(2):
            held[2, part] = held[2, part] + via[0, part]
        onward.append(go(held.at[2], row.at[0, 0], sem.at[2, 4], sem.at[3, 4], ahead))
        second.wait_recv()
        for part in range(2):
            held[5, part] = held[5, part] + via[1, part]
        onward.append(go(held.at[5], row.at[1, 1], sem.at[2, 5], sem.at[3, 5], behind))
        return onward

    def rows_total(held, row, half, part):
        return (
            held[6 + half, part].astype(F32)
            + row[0, half, part].astype(F32)
            + row[1, half, part].astype(F32)
        )

    def rows_across(onward, held, row, stage, landing, sem):
        for copy in onward:
            copy.wait_recv()
        for part in range(2):
            stage[part] = rows_total(held, row, 1 - high, part).astype(BF)
        return go(stage, landing, sem.at[2, 6], sem.at[3, 6], across)

    def rows_sum(last, held, row, landing, final, right, which):
        totals = [rows_total(held, row, high, part) for part in range(2)]
        last.wait_recv()
        for part in range(2):
            final[part] = (totals[part] + landing[part].astype(F32)).astype(BF)
        count = final.shape[1]
        copy = go(
            final.at[1 - core], right.at[pl.ds(count, count)],
            late_send.at[which], late_recv.at[which], sibling,
        )
        right[:count] = final[core]
        return copy


    starts = [sum(WIDTHS[:k]) for k in range(len(WIDTHS))]
    left_starts = [sum(LEFT[:k]) for k in range(4)]
    right_starts = [sum(RIGHT[:k]) for k in range(4)]
    acts = {}
    over_z, over_via, over_x = {}, {}, {}
    column_ahead = (me, low * 4 + (x + 1) % 4)
    column_behind = (me, low * 4 + (x + 3) % 4)

    def buffers(k):
        if k == DOWN:
            return d_z, d_x, d_via, pl.ds(0, D // 2)
        return from_z, from_x, via_x, pl.ds(starts[k], WIDTHS[k])

    def acts_start(index):
        left = pl.ds(left_starts[index], LEFT[index])
        right = pl.ds(right_starts[index], RIGHT[index])
        near = pl.ds(pl.multiple_of(core * RIGHT[index], 128), RIGHT[index])
        far = pl.ds(pl.multiple_of((1 - core) * RIGHT[index], 128), RIGHT[index])
        mine = pl.ds(0, TOK)
        theirs = pl.ds(TOK, TOK)
        acts[index] = (
            bring(lefts[index], left_all.at[mine, left], fill_sem.at[index, 0]),
            bring(rights[index].at[:, near], right_all.at[mine, right], fill_sem.at[index, 1]),
            go(
                lefts[index], left_all.at[theirs, left],
                act_send.at[index, 0], act_recv.at[index, 0], sibling,
            ),
            go(
                rights[index].at[:, far], right_all.at[theirs, right],
                act_send.at[index, 1], act_recv.at[index, 1], sibling,
            ),
        )

    def multiply(k, left_ref, right):
        landing, _, _, cut = buffers(k)
        for group in range(2):
            owners = pl.ds(4 * ((1 - low + group) % 2), 4)
            left = left_ref[owners].reshape(4 * PIECE, right.shape[0])
            kept[owners, :, cut] = (
                contract(left, right, ((1,), (0,))).astype(BF).reshape(4, PIECE, WIDTHS[k])
            )
            if group == 0:
                half = PIECE // 2
                over_z[k] = [
                    go(
                        kept.at[owners, pl.ds(side * half, half), cut],
                        landing.at[:, pl.ds(side * half, half), cut],
                        z_send.at[k, side],
                        z_recv.at[k, side],
                        device,
                    )
                    for side, device in enumerate((inside, outside))
                ]

    def make(index):
        near_left, near_right, far_left, far_right = acts[index]
        near_left.wait()
        near_right.wait()
        far_left.wait_recv()
        far_right.wait_recv()
        left = left_all[:, left_starts[index] : left_starts[index] + LEFT[index]].T
        right = right_all[:, right_starts[index] : right_starts[index] + RIGHT[index]]
        target = turned_one if index == 3 else turned
        target[...] = left.reshape(8, PIECE, 2 * TOK)
        multiply(index, target, right)

    def step_z(k):
        landing, _, _, cut = buffers(k)
        for copy in over_z[k]:
            copy.wait_recv()
        for column in range(4):
            landing[column, :, cut] = landing[column, :, cut] + kept[4 * low + column, :, cut]
        send_x(k)


    def send_x(k):
        landing, spread, via, cut = buffers(k)
        half = landing.shape[1] // 2
        upper, lower = pl.ds(0, half), pl.ds(half, half)
        away, front_column, back_column = (x + 2) % 4, (x + 1) % 4, (x + 3) % 4
        over_via[k] = (
            go(
                landing.at[away, upper, cut], via.at[0, :, cut],
                x_send.at[k, 0], x_recv.at[k, 0], column_ahead,
            ),
            go(
                landing.at[away, lower, cut], via.at[1, :, cut],
                x_send.at[k, 1], x_recv.at[k, 1], column_behind,
            ),
        )
        over_x[k] = [
            go(
                landing.at[front_column, lower, cut], spread.at[0, lower, cut],
                x_send.at[k, 2], x_recv.at[k, 2], column_ahead,
            ),
            go(
                landing.at[back_column, upper, cut], spread.at[1, upper, cut],
                x_send.at[k, 3], x_recv.at[k, 3], column_behind,
            ),
        ]

    def step_via(k):
        landing, spread, via, cut = buffers(k)
        half = landing.shape[1] // 2
        upper, lower = pl.ds(0, half), pl.ds(half, half)
        front_column, back_column = (x + 1) % 4, (x + 3) % 4
        over_via[k][0].wait_recv()
        landing[front_column, upper, cut] = landing[front_column, upper, cut] + via[0, :, cut]
        over_x[k].append(
            go(
                landing.at[front_column, upper, cut], spread.at[0, upper, cut],
                x_send.at[k, 4], x_recv.at[k, 4], column_ahead,
            )
        )
        over_via[k][1].wait_recv()
        landing[back_column, lower, cut] = landing[back_column, lower, cut] + via[1, :, cut]
        over_x[k].append(
            go(
                landing.at[back_column, lower, cut], spread.at[1, lower, cut],
                x_send.at[k, 5], x_recv.at[k, 5], column_behind,
            )
        )

    def step_x(k):
        landing, spread, _, cut = buffers(k)
        for copy in over_x[k]:
            copy.wait_recv()
        total = landing[x, :, cut].astype(F32)
        for spot in range(2):
            total = total + spread[spot, :, cut].astype(F32)
        total = total.astype(BF)
        half = D // 2
        if k == WIDE:
            for piece in range(8):
                packed[piece, :PIECE, :256] = total[:, piece * 256 : piece * 256 + 256]
        elif k == DOWN:
            for piece in range(8):
                for part in range(3):
                    packed[piece, part * 32 : part * 32 + 32, 256:] = total[
                        piece * 32 : piece * 32 + 32, part * 128 : part * 128 + 128
                    ]
        else:
            middle = PIECE // 2
            for upper in range(2):
                rows = total[upper * middle : upper * middle + middle, :]
                if k == CROSS_KV or k == SELF_KV:
                    for piece in range(2):
                        late_packed[(0 if k == CROSS_KV else 4) + 2 * piece + upper] = rows[
                            :, piece * half : piece * half + half
                        ]
                else:
                    packed[2 * k + upper, PIECE:, :] = rows


    def mate_device(mate):
        return (mate * 2 + core, shard)

    def ctx_start(which, source, landing):
        return [
            go(
                source.at[mate], landing.at[spot],
                ctx_send.at[which, spot], ctx_recv.at[which, spot], mate_device(mate),
            )
            for spot, mate in enumerate(mates)
        ]

    def ctx_sum(which, over, source, landing, final):
        total = source[rank].astype(F32)
        for spot in range(7):
            over[spot].wait_recv()
            total = total + landing[spot].astype(F32)
        final[rank, core] = total.astype(BF)
        own = final.at[rank, core]
        for spot, mate in enumerate(mates):
            go(own, own, ctx_send.at[which, 7 + spot], ctx_recv.at[which, 7 + rank], mate_device(mate))
        go(own, own, pass_send.at[which, 7], pass_recv.at[which, rank], sibling)

    def landed(ref, recv_sem):
        hop(ref, ref, pass_send.at[0, 0], recv_sem, *sibling).wait_recv()

    def ctx_pass(which, final):
        for spot, mate in enumerate(mates):
            block = final.at[mate, core]
            landed(block, ctx_recv.at[which, 7 + mate])
            go(block, block, pass_send.at[which, spot], pass_recv.at[which, mate], sibling)

    def ctx_done(which, final):
        for mate in [rank] + mates:
            landed(final.at[mate, 1 - core], pass_recv.at[which, mate])

    wide_cut = pl.ds(starts[WIDE], FF)
    down_copies = [bring(down_refs[0], d_z, bring_sem.at[0])] + [
        bring(down_refs[1 + side], down_add.at[side], bring_sem.at[1 + side]) for side in range(2)
    ]
    wide_copies = [bring(wide_refs[0], from_z.at[:, :, wide_cut], bring_sem.at[3])] + [
        bring(wide_refs[1 + side], wide_add.at[side], bring_sem.at[4 + side]) for side in range(2)
    ]
    s_copies = rows_start(dkv_ref, s_kept, s_core, s_sem)
    c_copies = rows_start(dckv_ref, c_kept, c_core, c_sem)
    for index in range(4):
        acts_start(index)
    state_near = bring(state_ref, state_all.at[pl.ds(0, ENC)], local_sem.at[0])
    state_far = go(
        state_ref, state_all.at[pl.ds(ENC, ENC)], late_send.at[2], late_recv.at[2], sibling
    )
    query_copy = bring(square_ref.at[:, :, pl.ds(0, D)], query_ref, bring_sem.at[6])
    for copy in down_copies:
        copy.wait()
    for side in range(2):
        for column in range(4):
            rows = slice(side * 128, side * 128 + 128)
            d_z[column, rows, :] = d_z[column, rows, :] + down_add[side, column]
    send_x(DOWN)
    for copy in wide_copies:
        copy.wait()
    for side in range(2):
        for column in range(4):
            rows = slice(side * 48, side * 48 + 48)
            from_z[column, rows, wide_cut] = from_z[column, rows, wide_cut] + wide_add[side, column]
    send_x(WIDE)
    s_state = rows_send(s_copies, s_kept, s_core, s_via, s_row, s_sem)
    make(0)
    make(1)
    s_onward = rows_via(s_state, s_kept, s_via, s_row, s_sem)
    c_state = rows_send(c_copies, c_kept, c_core, c_via, c_row, c_sem)
    make(2)
    make(3)
    step_via(DOWN)
    step_via(WIDE)
    for k in range(4):
        step_z(k)
    state_near.wait()
    state_far.wait_recv()
    turned_state[...] = state_all[...].T.reshape(8, PIECE, 2 * ENC)
    s_last = rows_across(s_onward, s_kept, s_row, s_stage, s_high, s_sem)
    c_onward = rows_via(c_state, c_kept, c_via, c_row, c_sem)
    for k in range(4):
        step_via(k)
    step_x(DOWN)
    step_x(WIDE)
    s_far = rows_sum(s_last, s_kept, s_row, s_high, s_fin, s_right, 0)
    for k in range(4):
        step_x(k)
    early = ctx_start(0, packed, from_ctx)
    s_far.wait_recv()
    multiply(SELF_KV, turned_one, s_right[...])
    c_last = rows_across(c_onward, c_kept, c_row, c_stage, c_high, c_sem)
    tokens = token_ref[...].astype(F32)
    d_kv = jnp.concatenate([s_fin[0], s_fin[1]], axis=1)
    query_copy.wait()
    grad = contract(dq_ref[...], query_ref[...].reshape(D, D), ((1,), (1,)))
    grad = grad + contract(d_kv, kv_ref[...], ((1,), (1,)))
    inverse = lax.rsqrt(jnp.mean(tokens * tokens, axis=-1, keepdims=True) + 1e-06)
    small_f32[...] = small_ref[...]
    line = jnp.sum(tokens * inverse * grad, axis=0, keepdims=True)
    for owner in range(8):
        small_f32[owner, 0:1, :96] = line[:, owner * 96 : owner * 96 + 96]
    sm_own[...] = small_f32[...].astype(BF)
    sm_over = go(sm_own, sm_core, sm_send.at[0], sm_recv.at[0], sibling)
    c_far = rows_sum(c_last, c_kept, c_row, c_high, c_fin, c_right, 1)
    c_far.wait_recv()
    multiply(CROSS_KV, turned_state, c_right[...])
    step_z(SELF_KV)
    sm_over.wait_recv()
    sm_own_sum = (sm_own[...].astype(F32) + sm_core[...].astype(F32)).astype(BF)
    sm_over.wait_send()
    sm_own[...] = sm_own_sum
    sm_inside = go(
        sm_own.at[pl.ds(4 * (1 - low), 4)], sm_z, sm_send.at[1], sm_recv.at[1], inside
    )
    ctx_sum(0, early, packed, from_ctx, land)
    step_z(CROSS_KV)
    step_via(SELF_KV)
    sm_inside.wait_recv()
    for column in range(4):
        sm_z[column] = sm_z[column] + sm_own[4 * low + column]
    sm_row = [
        go(
            sm_z.at[(x + spot + 1) % 4], sm_x.at[spot],
            sm_send.at[2 + spot], sm_recv.at[2 + spot], (me, others[spot]),
        )
        for spot in range(3)
    ]
    step_via(CROSS_KV)
    scaled = gain_ref[...] * grad
    mixed = jnp.mean(tokens * scaled, axis=-1, keepdims=True)
    decoder_ref[...] = (
        dmid_ref[...] + inverse * scaled - tokens * (inverse * inverse * inverse * mixed)
    )
    step_x(SELF_KV)
    step_x(CROSS_KV)
    late = ctx_start(1, late_packed, late_from)
    sm_sum = sm_z[x].astype(F32)
    for spot in range(3):
        sm_row[spot].wait_recv()
        sm_sum = sm_sum + sm_x[spot].astype(F32)
    sm_total[...] = sm_sum.astype(BF)
    sm_mates = [
        go(sm_total, sm_ctx.at[spot], sm_send.at[5 + spot], sm_recv.at[5 + spot], mate_device(mate))
        for spot, mate in enumerate(mates)
    ]
    ctx_pass(0, land)
    ctx_sum(1, late, late_packed, late_from, late_land)
    d_ckv = jnp.concatenate([c_fin[0], c_fin[1]], axis=1)
    encoder_ref[...] = contract(d_ckv, ckv_ref[...], ((1,), (1,)))
    sm_sum = sm_total[...].astype(F32)
    for spot in range(7):
        sm_mates[spot].wait_recv()
        sm_sum = sm_sum + sm_ctx[spot].astype(F32)
    small_out[...] = sm_sum
    ctx_done(0, land)
    early_out[...] = land[...]
    ctx_pass(1, late_land)
    ctx_done(1, late_land)
    late_out[...] = late_land[...]
    for copy in sends:
        if copy is not sm_over:
            copy.wait_send()


def unpack_kernel(early, late, *refs):
    square_refs = refs[:8]
    gate_ref, up_ref, down_ref = refs[8:]
    half = D // 2
    middle = PIECE // 2
    for side in range(2):
        columns = slice(side * half, side * half + half)
        for upper in range(2):
            rows = slice(upper * middle, upper * middle + middle)
            for k in range(4):
                square_refs[k][rows, columns] = early[2 * k + upper, side, PIECE:, :].astype(F32)
            for k in range(2):
                for piece in range(2):
                    square_refs[4 + 2 * k + side][rows, piece * half : piece * half + half] = late[
                        4 * k + 2 * piece + upper, side
                    ].astype(F32)
        target = up_ref if side else gate_ref
        for piece in range(8):
            target[:, piece * 256 : piece * 256 + 256] = early[piece, side, :PIECE, :256].astype(F32)
            for part in range(3):
                down_ref[
                    piece * 32 : piece * 32 + 32,
                    side * half + part * 128 : side * half + part * 128 + 128,
                ] = early[piece, side, part * 32 : part * 32 + 32, 256:].astype(F32)


def unpack(early, late):
    outs = (
        [jax.ShapeDtypeStruct((PIECE, D), F32)] * 8
        + [jax.ShapeDtypeStruct((PIECE, FF), F32)] * 2
        + [jax.ShapeDtypeStruct((FF // 8, D), F32)]
    )
    return pl.pallas_call(
        unpack_kernel,
        out_shape=outs,
        in_specs=[pl.BlockSpec(memory_space=pltpu.VMEM)] * 2,
        out_specs=[pl.BlockSpec(memory_space=pltpu.VMEM)] * len(outs),
        compiler_params=pltpu.CompilerParams(vmem_limit_bytes=24 * MIB),
        name="unpack",
    )(early, late)


def finish(far, near, collective_id):
    dma = pltpu.SemaphoreType.DMA

    def rows(count):
        return [
            pltpu.VMEM((8, 2, count, D), BF),
            pltpu.VMEM((8, 2, count, D), BF),
            pltpu.VMEM((2, 2, 2, count, D), BF),
            pltpu.VMEM((2, 2, count, D), BF),
            pltpu.VMEM((2, count, D), BF),
            pltpu.VMEM((2, count, D), BF),
            pltpu.VMEM((2, count, D), BF),
        ]

    outs = [
        jax.ShapeDtypeStruct((8, 2, 3 * PIECE // 2, D // 2), BF),
        jax.ShapeDtypeStruct((8, 2, PIECE // 2, D // 2), BF),
        jax.ShapeDtypeStruct((16, 128), F32),
        jax.ShapeDtypeStruct((TOK, D), F32),
        jax.ShapeDtypeStruct((ENC, D), F32),
    ]
    return pl.pallas_call(
        finish_kernel,
        out_shape=outs,
        in_specs=[pl.BlockSpec(memory_space=pl.ANY)] * len(far)
        + [pl.BlockSpec(memory_space=pltpu.VMEM)] * len(near),
        out_specs=[pl.BlockSpec(memory_space=pltpu.VMEM)] * len(outs),
        scratch_shapes=[
            pltpu.VMEM((2 * TOK, sum(LEFT)), BF),
            pltpu.VMEM((2 * TOK, sum(RIGHT)), BF),
            pltpu.VMEM((8, PIECE, 2 * TOK), BF),
            pltpu.VMEM((8, PIECE, 2 * TOK), BF),
            pltpu.VMEM((8, PIECE, 2 * ENC), BF),
            pltpu.VMEM((2 * ENC, D), BF),
            pltpu.VMEM((2 * TOK, D), BF),
            pltpu.VMEM((2 * ENC, D), BF),
            pltpu.VMEM((8, PIECE, SPAN - FF), BF),
            pltpu.VMEM((4, PIECE, SPAN), BF),
            pltpu.VMEM((2, PIECE, SPAN), BF),
            pltpu.VMEM((2, PIECE // 2, SPAN), BF),
            pltpu.VMEM((4, FF // 8, D // 2), BF),
            pltpu.VMEM((2, FF // 8, D // 2), BF),
            pltpu.VMEM((2, FF // 16, D // 2), BF),
        ]
        + rows(TOK)
        + rows(ENC)
        + [
            pltpu.VMEM((8, 16, 128), F32),
            pltpu.VMEM((8, 16, 128), BF),
            pltpu.VMEM((8, 16, 128), BF),
            pltpu.VMEM((4, 16, 128), BF),
            pltpu.VMEM((3, 16, 128), BF),
            pltpu.VMEM((7, 16, 128), BF),
            pltpu.VMEM((16, 128), BF),
            pltpu.VMEM((8, 3 * PIECE // 2, D // 2), BF),
            pltpu.VMEM((7, 3 * PIECE // 2, D // 2), BF),
            pltpu.VMEM((8, 2, 3 * PIECE // 2, D // 2), BF),
            pltpu.VMEM((8, PIECE // 2, D // 2), BF),
            pltpu.VMEM((7, PIECE // 2, D // 2), BF),
            pltpu.VMEM((8, 2, PIECE // 2, D // 2), BF),
            pltpu.VMEM((2, 4, PIECE // 2, FF), BF),
            pltpu.VMEM((2, 4, FF // 16, D // 2), BF),
            pltpu.VMEM((8, PIECE, D), BF),
            dma((7,)),
            dma((5, 7)),
            dma((5, 7)),
            dma((4, 2)),
            dma((4, 2)),
            dma((4, 2)),
            dma((3,)),
            dma((3,)),
            dma((CHUNKS, 2)),
            dma((CHUNKS, 2)),
            dma((CHUNKS, 6)),
            dma((CHUNKS, 6)),
            dma((2, 14)),
            dma((2, 15)),
            dma((2, 8)),
            dma((2, 8)),
            dma((12,)),
            dma((12,)),
            dma((3,)),
        ],
        compiler_params=pltpu.CompilerParams(
            collective_id=collective_id, has_side_effects=True, vmem_limit_bytes=62 * MIB
        ),
        name="finish_gradients",
    )(*far, *near)


def backward_kernel(biased, *refs):
    if biased:
        class_ref, near_ref, q_ref, k_ref, v_ref, g_ref, total_ref, tile_ref = refs[:8]
        dq_ref, dkv_ref, strip_ref, share_ref, slope_ref, share_low, slope_low = refs[8:]
    else:
        q_ref, k_ref, v_ref, g_ref, total_ref = refs[:5]
        dq_ref, dkv_ref, share_ref, slope_ref, share_low, slope_low = refs[5:]
    chunks = share_ref.shape[0]
    queries = split_heads(q_ref[...])
    grads = split_heads(g_ref[...])
    totals = total_ref[0, 0:1]
    inner = jnp.zeros((8, 2 * TOK), F32)
    for j in range(chunks):
        scores = contract(key_chunk(k_ref, j), queries, ((1,), (1,)))
        if biased:
            scores = scores + bias_chunk(class_ref, tile_ref, j)
        shares = jnp.exp(scores - totals)
        slopes = contract(key_chunk(v_ref, j), grads, ((1,), (1,)))
        inner = inner + fold(shares * slopes, jnp.sum)
        share_ref[j] = shares
        slope_ref[j] = slopes
        share_low[j] = shares.astype(BF)
    inner = jnp.sum(inner, axis=0, keepdims=True)
    for j in range(chunks):
        grad = share_ref[j] * (slope_ref[j] - inner)
        if biased:
            slope_ref[j] = grad
        slope_low[j] = grad.astype(BF)
    keys = jnp.concatenate([key_chunk(k_ref, j) for j in range(chunks)], axis=0)
    low = slope_low[...].reshape(-1, 2 * TOK)
    dq_ref[...] = join_heads(contract(keys, low, ((0,), (0,)))).astype(BF)
    shape = dkv_ref.shape
    block = (shape[0], shape[2], shape[3])
    dkv_ref[:, 0] = contract(low, queries, ((1,), (0,))).astype(BF).reshape(block)
    dkv_ref[:, 1] = (
        contract(share_low[...].reshape(-1, 2 * TOK), grads, ((1,), (0,))).astype(BF).reshape(block)
    )
    if biased:
        lane = lax.broadcasted_iota(jnp.int32, (HALF, TOK), 1)
        for gap in range(3):
            pieces = []
            for half in range(2):
                spot = near_ref[half, gap]
                held = slope_ref[jnp.maximum(spot, 0) // 2, pl.ds(
                    pl.multiple_of((jnp.maximum(spot, 0) % 2) * HALF, HALF), HALF)]
                pieces.append(jnp.where(spot >= 0, held, jnp.zeros_like(held)))
            for head in range(2):
                cut = slice(head * TOK, (head + 1) * TOK)
                strip_ref[head, gap] = jnp.where(lane < HALF, pieces[0][:, cut], pieces[1][:, cut])


def pair_columns(pair):
    return (0, pair)


def kv_spec(rows, row_block, part):
    return pl.BlockSpec(
        (N_CTX, 1, rows, 2 * HEAD_DIM), lambda pair: (0, part, row_block, pair)
    )


SMEM_SPEC = pl.BlockSpec(memory_space=pltpu.SMEM)
TILE_SPEC = pl.BlockSpec((2, 5, HALF, TOK), lambda pair: (pair, 0, 0, 0))
TOTAL_SPEC = pl.BlockSpec((1, 8, 2 * TOK), lambda pair: (pair, 0, 0))
ROW_SPEC = pl.BlockSpec((TOK, 2 * HEAD_DIM), pair_columns)
LOCAL = pltpu.CompilerParams(vmem_limit_bytes=48 * MIB)


def attend_back(queries, gathered, grads, totals, rows, row_block, classes=None, near=None, tiles=None):
    biased = classes is not None
    chunks = N_CTX * rows // TOK
    specs = [ROW_SPEC, kv_spec(rows, row_block, 0), kv_spec(rows, row_block, 1), ROW_SPEC, TOTAL_SPEC]
    operands = [queries, gathered, gathered, grads, totals]
    out_specs = [
        ROW_SPEC,
        pl.BlockSpec((N_CTX, 2, rows, 2 * HEAD_DIM), lambda pair: (0, 0, 0, pair)),
    ]
    out_shape = [
        jax.ShapeDtypeStruct((TOK, D), BF),
        jax.ShapeDtypeStruct((N_CTX, 2, rows, D), BF),
    ]
    if biased:
        specs = [SMEM_SPEC, SMEM_SPEC] + specs + [TILE_SPEC]
        operands = [classes, near] + operands + [tiles]
        out_specs.append(pl.BlockSpec((2, 3, HALF, TOK), lambda pair: (pair, 0, 0, 0)))
        out_shape.append(jax.ShapeDtypeStruct((HEADS, 3, HALF, TOK), F32))
    return pl.pallas_call(
        functools.partial(backward_kernel, biased),
        grid=(PAIRS,),
        in_specs=specs,
        out_specs=out_specs,
        out_shape=out_shape,
        scratch_shapes=[
            pltpu.VMEM((chunks, TOK, 2 * TOK), F32),
            pltpu.VMEM((chunks, TOK, 2 * TOK), F32),
            pltpu.VMEM((chunks, TOK, 2 * TOK), BF),
            pltpu.VMEM((chunks, TOK, 2 * TOK), BF),
        ],
        compiler_params=LOCAL,
        cost_estimate=pl.CostEstimate(flops=1000, bytes_accessed=1000, transcendentals=0),
        name="attend_self_back" if biased else "attend_cross_back",
    )(*operands)


def matmul(left, right):
    return jnp.dot(left, right, preferred_element_type=F32)


def transposed_left(left, right):
    return contract(left, right, ((0,), (0,)))


def transposed_right(left, right):
    return contract(left, right, ((1,), (1,)))


def rms_scaled(values, gain):
    inverse = lax.rsqrt(jnp.mean(values * values, axis=-1, keepdims=True) + 1e-06)
    return (values * inverse * gain).astype(BF)


def rms_back(values, gain, grad):
    inverse = lax.rsqrt(jnp.mean(values * values, axis=-1, keepdims=True) + 1e-06)
    scaled = gain * grad
    mixed = jnp.mean(values * scaled, axis=-1, keepdims=True)
    grad_values = inverse * scaled - values * (inverse * inverse * inverse * mixed)
    return grad_values, jnp.sum(values * inverse * grad, axis=0)


def near_hot():
    shape = (REACH, 3 * HALF * HALF)
    spot = lax.broadcasted_iota(jnp.int32, shape, 1)
    gap = spot // (HALF * HALF)
    key = (spot // HALF) % HALF
    row = spot % HALF
    distance = jnp.clip(HALF * gap + row - key, 0, REACH - 1)
    return (distance == lax.broadcasted_iota(jnp.int32, shape, 0)).astype(BF)


def bias_sums(strips):
    tiles = (strips[..., :HALF] + strips[..., HALF:]).reshape(HEADS, -1)
    high = tiles.astype(BF)
    low = (tiles - high.astype(F32)).astype(BF)
    hot = near_hot()
    sums = transposed_right(high, hot) + transposed_right(low, hot)
    far = -jnp.sum(sums[:, :-1], axis=1, keepdims=True)
    return jnp.concatenate([sums[:, :-1], far], axis=1)


def swap(values, move):
    perm = []
    for ctx in range(N_CTX):
        for shard in range(8):
            there, owner = move(ctx, shard)
            perm.append((ctx * 8 + shard, there * 8 + owner))
    return lax.ppermute(values, ("ctx", "fsdp"), perm)


def over_z(mine, upper, lower):
    inner = swap(upper, lambda ctx, shard: (ctx, (shard + 4) % 8))
    outer = swap(lower, lambda ctx, shard: (ctx ^ 2, (shard + 4) % 8))
    return mine, inner, outer


def body(
    decoder_in,
    encoder_states,
    out_grad,
    block_pairs,
    bucket_table,
    gain_self,
    self_query,
    self_key,
    self_value,
    self_out,
    position_bias,
    gain_cross,
    cross_query,
    cross_key,
    cross_value,
    cross_out,
    gain_feed,
    feed_gate,
    feed_up,
    feed_down,
):
    me = lax.axis_index("ctx")
    rows = self_query.shape[0]
    small = jnp.concatenate(
        [
            jnp.pad(jnp.stack([gain_self, gain_cross, gain_feed]), ((0, 0), (0, 128 - rows))),
            jnp.pad(position_bias, ((0, 9), (0, 128 - HEADS))),
        ],
        axis=0,
    )
    (
        kv_one, kv_two, square, gains, normed_one, queries, tiles, attended, self_totals, mid_one,
        normed_two, cross_queries, cross_attended, cross_totals, block_out, d_mid_two,
        cross_branch, d_cross_attended, grad_norm_three, *feed_parts, classes, near, self_kv,
        cross_kv,
    ) = front(
        [
            self_key, self_value, cross_key, cross_value,
            self_query, self_out, cross_query, cross_out,
            feed_gate, feed_up, feed_down,
        ],
        [
            small, decoder_in[0], encoder_states[0], out_grad[0], bucket_table[None, :], block_pairs,
        ],
        0,
    )
    kv_one = kv_one.reshape(D, 2 * D)
    kv_two = kv_two.reshape(D, 2 * D)
    out_one, query_two = (square.reshape(D, 4 * D)[:, k * D : k * D + D] for k in (1, 2))
    norm_one, norm_two = gains[0:1], gains[1:2]
    bucket_hot = (bucket_table[:, None] == jnp.arange(32, dtype=jnp.int32)[None, :]).astype(BF)
    tokens = decoder_in[0].astype(F32)
    states = encoder_states[0]
    upstream = out_grad[0]
    feed_parts = [over_z(*feed_parts[:3]), over_z(*feed_parts[3:])]
    d_cross_queries, d_cross_kv_all = attend_back(
        cross_queries, cross_kv, d_cross_attended, cross_totals, ENC, 0
    )
    d_normed_two = transposed_right(d_cross_queries, query_two)
    part_two, grad_norm_two = rms_back(mid_one, norm_two, d_normed_two)
    d_mid_one = d_mid_two + part_two
    self_branch = d_mid_one.astype(BF)
    d_attended = transposed_right(self_branch, out_one).astype(BF)
    feed_parts[1], d_attended = lax.optimization_barrier((feed_parts[1], d_attended))
    d_queries, d_kv_all, strips = attend_back(
        queries, self_kv, d_attended, self_totals, TOK, 0, classes, near, tiles
    )
    feed_parts, d_queries, d_kv_all, strips = lax.optimization_barrier(
        (feed_parts, d_queries, d_kv_all, strips)
    )
    grad_table = matmul(bias_sums(strips), bucket_hot.astype(F32)).T.reshape(8, 4, HEADS)
    grad_gains = jnp.stack([grad_norm_two, grad_norm_three[0]]).reshape(2, 8, rows)
    grad_small = jnp.concatenate(
        [
            jnp.zeros((8, 1, 128), F32),
            jnp.pad(jnp.transpose(grad_gains, (1, 0, 2)), ((0, 0), (0, 0), (0, 128 - rows))),
            jnp.pad(grad_table, ((0, 0), (0, 9), (0, 128 - HEADS))),
        ],
        axis=1,
    )
    done = finish(
        [
            cross_attended, normed_two, attended, normed_one,
            cross_branch, d_cross_queries, self_branch, d_queries,
            *feed_parts[0],
            *feed_parts[1],
            d_kv_all.reshape(8, 2, 2, TOK, D),
            d_cross_kv_all.reshape(8, 2, 2, ENC, D),
            square,
        ],
        [
            states,
            kv_one,
            kv_two,
            d_queries,
            d_mid_one,
            decoder_in[0],
            norm_one,
            grad_small,
        ],
        3,
    )
    early, late, extras, grad_decoder, grad_encoder = done
    (
        grad_out_two, grad_query_two, grad_out_one, grad_query_one,
        grad_key_two, grad_value_two, grad_key_one, grad_value_one,
        grad_gate, grad_up, grad_down,
    ) = unpack(early, late)
    return (
        block_out[None],
        grad_decoder[None],
        grad_encoder[None],
        extras[0, :rows],
        grad_query_one,
        grad_key_one,
        grad_value_one,
        grad_out_one,
        extras[3:7, :HEADS],
        extras[1, :rows],
        grad_query_two,
        grad_key_two,
        grad_value_two,
        grad_out_two,
        extras[2, :rows],
        grad_gate,
        grad_up,
        grad_down,
    )


def solution(mesh):
    tokens = P("fsdp", "ctx", None)
    matrix = P("fsdp", None)
    vector = P("fsdp")
    weights = (
        (vector,) + (matrix,) * 5 + (vector,) + (matrix,) * 4 + (vector,) + (matrix,) * 3
    )
    return jax.shard_map(
        body,
        mesh=mesh,
        in_specs=(tokens,) * 3 + (P(), P()) + weights,
        out_specs=(tokens,) * 3 + weights,
        check_vma=False,
    )
```

profile of v0, /device:TPU:1, one launch (start us, length us, event | category | flops | bytes accessed | tf_op | source)
XLA Modules:
  0.0 279.2 jit_solution(695311190479924842)
XLA Ops:
  0.7 0.7 fusion.37
  1.4 1.3 fusion.32.refs_11_
  2.6 104.0 %front.1 = (bf16[8,96,1536]{2,1,0:T(8,128)(2,1)}, bf16[8,96,1536]{2,1,0:T(8,128)(2,1)}, bf16[8,96,3072]{2,1,0:T(8,128)(2,1)}, f32[3,768]{1,0:T(4,128)}, bf16[128...) custom-call(bf16[96,768]{1,0:T(8,128)(2,1)} %refs_0_.1, ...), custom_call_target="tpu_custom_call" | custom-call | tf_op jit(solution)/shard_map/front/pallas_call | solution.py:541
  106.7 1.1 collective-permute-start.1
  107.9 0.8 collective-permute-start.2
  108.6 1.6 collective-permute-start.3
  110.4 1.1 multiply_reduce_fusion.2
  111.5 1.4 fusion.42
  112.9 0.9 copy-done.7
  113.8 0.9 copy-done.8
  114.7 0.8 copy-done.10
  115.5 8.3 %attend_cross_back.1 = (bf16[128,768]{1,0:T(8,128)(2,1)S(1)}, bf16[16,2,64,768]{3,2,1,0:T(8,128)(2,1)S(1)}) custom-call(bf16[128,768]{1,0:T(8,128)(2,1)S(1)} %copy-done.7, bf16[16,2,64,768]{3,2,1,0:T(8,128)(2,1)} %get-tuple-element.88.refs_1_.refs_2_, bf16[16,2,64,768]{3,2,1,0:T(8,128)(2,1)} %get-tuple-element.88.refs_1_.refs_2_, ...), custom_call_target="tpu_custom_call" | custom-call | flops 1000 | bytes 1000 | tf_op jit(solution)/shard_map/attend_cross_back/pallas_call | solution.py:1277
  123.8 2.9 %multiply_reduce_fusion = (f32[768]{0:T(1024)S(1)}, f32[128]{0:T(128)S(1)}, f32[128,768]{1,0:T(8,128)S(1)}) fusion(f32[128,768]{1,0:T(8,128)S(1)} %copy-done.14, f32[128]{0:T(128)S(1)} %add_rsqrt_fusion, f32[768]{0:T(1024)S(1)} %get-tuple-element.151, bf16[128,768]{1,0:T(8,128)(2,1)S(1)} %get-tuple-element.91.refs_5_, bf16[768,3072]{1,0:T(8,128)(2,1)} %bitcast.35), kind=kOutput, calls=%fused_computation.17 | convolution fusion | flops 151583872 | bytes 2169856 | tf_op jit(solution)/shard_map/dot_general | solution.py:52
  126.8 2.2 fusion.2
  129.0 0.9 fusion.41
  130.1 1.8 fusion.8.refs_5_
  131.9 3.0 %collective-permute-done.2.refs_12_ = bf16[4,128,384]{2,1,0:T(8,128)(2,1)} collective-permute-done((bf16[4,128,384]{2,1,0:T(8,128)(2,1)}, bf16[4,128,384]{2,1,0:T(8,128)(2,1)}, u32[]{:S(2)}, u32[]{:S(2)}) %collective-permute-start.2) | collective-permute-done | bytes 393248 | tf_op jit(solution)/shard_map/ppermute | solution.py:1346
  134.9 1.3 collective-permute-done.3.refs_13_
  136.2 13.4 %attend_self_back.1 = (bf16[128,768]{1,0:T(8,128)(2,1)S(1)}, bf16[16,2,128,768]{3,2,1,0:T(8,128)(2,1)}, f32[12,3,64,128]{3,2,1,0:T(8,128)S(1)}) custom-call(s32[2,32]{1,0:T(2,128)S(1)} %copy-done.11, s32[2,3]{1,0:T(2,128)S(1)} %copy-done.12, bf16[128,768]{1,0:T(8,128)(2,1)S(1)} %copy-done.6, bf16[16,2,128,768]{3,2,1,0:T(8,128)(2,1)} %get-tuple-element.108.refs_3_.refs_4_, ...), custom_call_target="tpu_custom_call" | custom-call | flops 1000 | bytes 1000 | tf_op jit(solution)/shard_map/attend_self_back/pallas_call | solution.py:1277
  150.3 0.9 copy-done.16
  152.6 0.9 fusion.11
  153.5 0.9 fusion.13
  154.9 0.7 select_maximum_fusion.refs_24_
  155.7 114.0 %finish_gradients.1 = (bf16[8,2,144,384]{3,2,1,0:T(8,128)(2,1)}, bf16[8,2,48,384]{3,2,1,0:T(8,128)(2,1)}, f32[16,128]{1,0:T(8,128)}, f32[128,768]{1,0:T(8,128)}, f32[64,768]{1,0:T(8,128)}) custom-call(bf16[128,768]{1,0:T(8,128)(2,1)} %get-tuple-element.82.refs_0_, bf16[128,768]{1,0:T(8,128)(2,1)} %get-tuple-element.83.refs_1_, ...), custom_call_target="tpu_custom_call" | custom-call | tf_op jit(solution)/shard_map/finish_gradients/pallas_call | solution.py:1122
  269.7 1.3 slice_bitcast_fusion
  271.0 1.2 slice.42
  272.2 1.5 copy-done.2
  273.7 1.1 copy-done.4
  274.8 2.2 unpack.1
  277.0 0.7 copy.47
  277.8 0.7 copy.48
  278.5 0.7 copy.49
  (61 shorter events, 3.0 us)
Async XLA Ops:
  106.7 43.7 %collective-permute-start = (bf16[4,48,2048]{2,1,0:T(8,128)(2,1)}, bf16[4,48,2048]{2,1,0:T(8,128)(2,1)S(1)}, u32[]{:S(2)}, u32[]{:S(2)}) collective-permute-start(bf16[4,48,2048]{2,1,0:T(8,128)(2,1)} %get-tuple-element.97), channel_id=1, source_target_pairs={{0,4},{1,5},{2,6},{3,7},{4,0},{5,1},{6,2},{7,3},{8,12},{9,13},{10,... | collective-permute-start | bytes 2359304 | tf_op jit(solution)/shard_map/ppermute | solution.py:1346
  106.7 43.6 %collective-permute-start.1 = (bf16[4,48,2048]{2,1,0:T(8,128)(2,1)}, bf16[4,48,2048]{2,1,0:T(8,128)(2,1)}, u32[]{:S(2)}, u32[]{:S(2)}) collective-permute-start(bf16[4,48,2048]{2,1,0:T(8,128)(2,1)} %get-tuple-element.98), channel_id=1, source_target_pairs={{0,20},{1,21},{2,22},{3,23},{4,16},{5,17},{6,18},{7,19},{8,28},{9,... | collective-permute-start | bytes 2359304 | tf_op jit(solution)/shard_map/ppermute | solution.py:1346
  107.9 27.0 %collective-permute-start.2 = (bf16[4,128,384]{2,1,0:T(8,128)(2,1)}, bf16[4,128,384]{2,1,0:T(8,128)(2,1)}, u32[]{:S(2)}, u32[]{:S(2)}) collective-permute-start(bf16[4,128,384]{2,1,0:T(8,128)(2,1)} %get-tuple-element.100), channel_id=1, source_target_pairs={{0,4},{1,5},{2,6},{3,7},{4,0},{5,1},{6,2},{7,3},{8,12},{9,13},{10,... | collective-permute-start | bytes 1179656 | tf_op jit(solution)/shard_map/ppermute | solution.py:1346
  108.6 27.6 %collective-permute-start.3 = (bf16[4,128,384]{2,1,0:T(8,128)(2,1)}, bf16[4,128,384]{2,1,0:T(8,128)(2,1)}, u32[]{:S(2)}, u32[]{:S(2)}) collective-permute-start(bf16[4,128,384]{2,1,0:T(8,128)(2,1)} %get-tuple-element.101), channel_id=1, source_target_pairs={{0,20},{1,21},{2,22},{3,23},{4,16},{5,17},{6,18},{7,19},{8,28},{9,... | collective-permute-start | bytes 1179656 | tf_op jit(solution)/shard_map/ppermute | solution.py:1346
  112.9 0.9 copy-start.7
  113.8 0.9 copy-start.8
  114.7 0.8 copy-start.10
  115.5 8.3 %copy-start.14 = (f32[128,768]{1,0:T(8,128)S(1)}, f32[128,768]{1,0:T(8,128)}, u32[]{:S(2)}) copy-start(f32[128,768]{1,0:T(8,128)} %get-tuple-element.93) | copy-start | bytes 1179652
  123.8 6.1 %copy-start = (bf16[16,2,64,768]{3,2,1,0:T(8,128)(2,1)}, bf16[16,2,64,768]{3,2,1,0:T(8,128)(2,1)S(1)}, u32[]{:S(2)}) copy-start(bf16[16,2,64,768]{3,2,1,0:T(8,128)(2,1)S(1)} %get-tuple-element.123) | copy-start | bytes 9437188
  123.8 6.1 %copy-start.5 = (bf16[128,768]{1,0:T(8,128)(2,1)}, bf16[128,768]{1,0:T(8,128)(2,1)S(1)}, u32[]{:S(2)}) copy-start(bf16[128,768]{1,0:T(8,128)(2,1)S(1)} %get-tuple-element.91.refs_5_) | copy-start | bytes 589828
  123.8 5.2 %copy-start.19 = (f32[128,768]{1,0:T(8,128)S(1)}, f32[128,768]{1,0:T(8,128)}, u32[]{:S(2)}) copy-start(f32[128,768]{1,0:T(8,128)} %get-tuple-element.92) | copy-start | bytes 1179652
  126.8 3.1 %copy-start.21 = (f32[1,768]{1,0:T(1,128)S(1)}, f32[1,768]{1,0:T(1,128)}, u32[]{:S(2)}) copy-start(f32[1,768]{1,0:T(1,128)} %get-tuple-element.126) | copy-start | bytes 9220
  126.8 9.4 %copy-start.1 = (f32[12,5,64,128]{3,2,1,0:T(8,128)S(1)}, f32[12,5,64,128]{3,2,1,0:T(8,128)}, u32[]{:S(2)}) copy-start(f32[12,5,64,128]{3,2,1,0:T(8,128)} %get-tuple-element.111.refs_7_) | copy-start | bytes 5898244
  126.8 9.4 %copy-start.6 = (bf16[128,768]{1,0:T(8,128)(2,1)S(1)}, bf16[128,768]{1,0:T(8,128)(2,1)}, u32[]{:S(2)}) copy-start(bf16[128,768]{1,0:T(8,128)(2,1)} %get-tuple-element.107.refs_2_) | copy-start | bytes 589828
  126.8 9.4 %copy-start.9 = (f32[6,8,256]{2,1,0:T(8,128)S(1)}, f32[6,8,256]{2,1,0:T(8,128)}, u32[]{:S(2)}) copy-start(f32[6,8,256]{2,1,0:T(8,128)} %get-tuple-element.110.refs_6_) | copy-start | bytes 147460
  126.8 9.4 %copy-start.11 = (s32[2,32]{1,0:T(2,128)S(1)}, s32[2,32]{1,0:T(2,128)}, u32[]{:S(2)}) copy-start(s32[2,32]{1,0:T(2,128)} %get-tuple-element.105.refs_0_) | copy-start | bytes 772
  126.8 9.4 %copy-start.12 = (s32[2,3]{1,0:T(2,128)S(1)}, s32[2,3]{1,0:T(2,128)}, u32[]{:S(2)}) copy-start(s32[2,3]{1,0:T(2,128)} %get-tuple-element.106.refs_1_) | copy-start | bytes 76
  129.9 19.7 %copy-start.15 = (bf16[128,768]{1,0:T(8,128)(2,1)}, bf16[128,768]{1,0:T(8,128)(2,1)S(1)}, u32[]{:S(2)}) copy-start(bf16[128,768]{1,0:T(8,128)(2,1)S(1)} %get-tuple-element.148.refs_6_) | copy-start | bytes 589828
  149.6 0.7 copy-start.3
  150.3 0.9 copy-start.16
  151.2 1.4 copy-start.13
  152.6 2.1 copy-start.22
  155.7 121.4 %copy-start.17 = (f32[128,768]{1,0:T(8,128)S(1)}, f32[128,768]{1,0:T(8,128)}, u32[]{:S(2)}) copy-start(f32[128,768]{1,0:T(8,128)} %get-tuple-element.81) | copy-start | bytes 1179652
  272.2 1.5 copy-start.2
  273.7 1.1 copy-start.4
  274.8 3.0 %copy-start.18 = (f32[128,768]{1,0:T(8,128)S(1)}, f32[128,768]{1,0:T(8,128)}, u32[]{:S(2)}) copy-start(f32[128,768]{1,0:T(8,128)} %get-tuple-element.128) | copy-start | bytes 1179652
  274.8 3.7 %copy-start.20 = (f32[64,768]{1,0:T(8,128)S(1)}, f32[64,768]{1,0:T(8,128)}, u32[]{:S(2)}) copy-start(f32[64,768]{1,0:T(8,128)} %get-tuple-element.129) | copy-start | bytes 589828
where the time goes:
time: 280 us; the launch traced here: 279 us
  Pallas kernels  242 us (86%)
  local copies, waits for them, and re-layouts  14.2 us (5%)
  other arithmetic  7.43 us (3%)
  matrix products  6.85 us (2%)
  waiting for transfers between devices  4.3 us (2%)
  starting transfers between devices  3.61 us (1%)
    pallas_call x1, Pallas kernels, finish(): pl.pallas_call(finish_kernel, out_shape=outs, in_specs=[pl.BlockSpec(memo...  114 us
    pallas_call x1, Pallas kernels, front(): pl.pallas_call(front_kernel, out_shape=[jax.ShapeDtypeStruct(pack, BF) fo...  104 us
    pallas_call x2, Pallas kernels, attend_back(): pl.pallas_call(functools.partial(backward_kernel, biased), grid=(PAIRS,),...  21.7 us
    unnamed x49, local copies, waits for them, and re-layouts  9.6 us
    dot_general x4, matrix products, contract(): lax.dot_general(left, right, (dims, ((), ())), preferred_element_type=F32)  6.58 us
  transfers between devices with their start and end apart: 4, of which 2 were waited for; matrix products, arithmetic and copies ran while one was open for 4% of the time, Pallas kernels for 8%

commit v1 on v0

--- a/solution.py
+++ b/solution.py
@@ -195,6 +195,7 @@
     pl.semaphore_wait(barrier, len(devices))
 
 
+Z_FIRST = 4
 ROOT = (2.0 / 3.141592653589793) ** 0.5
 PACKS = ((0, 1), (2, 3), (4, 5, 6, 7), (8, 9), (10,))
 
@@ -204,16 +205,17 @@
     small_ref, token_ref, state_ref, upstream_ref, bucket_ref, pairs_ref = refs[11:17]
     results = refs[17:20]
     (
-        gain_out, normed_out, query_out, tile_ref, attended_ref, total_ref, mid_one_ref,
+        gain_out, normed_out, query_out, tile_result, attended_ref, total_ref, mid_one_ref,
         normed_two_ref, cross_query_ref, cross_attended_ref, cross_total_ref,
         block_ref, d_mid_ref, branch_ref, d_cross_ref, gain_grad_ref,
-        wide_mine, wide_inner, wide_outer, tall_mine, tall_inner, tall_outer,
+        wide_mine_out, wide_inner_out, wide_outer_out, tall_mine_out, tall_inner_out, tall_outer_out,
         class_ref, near_ref, self_result, cross_result,
     ) = refs[20:46]
     targets = refs[46:51]
     (
         self_out_ref, cross_out_ref, landing, self_ref, cross_ref, score_ref, share_ref,
-        feed_left, feed_right, slope_ref, turned, turned_hidden,
+        feed_left, feed_right, slope_ref, turned, turned_hidden, tile_ref,
+        wide_mine, wide_inner, wide_outer, tall_mine, tall_inner, tall_outer,
         send_sem, x_sem, z_sem, core_sem,
         fill_sem, small_sem, self_sem, cross_sem, feed_sem, local_sem,
     ) = refs[51:]
@@ -286,9 +288,10 @@
             owner = low * 4 + (x + 3 - spot) % 4
             block = part(k, owner, core)
             arrived(block, x_sem.at[k, spot])
-            for side, device in enumerate((inside, outside)):
-                piece = part(k, owner, core, side)
-                send(piece, piece, z_sem.at[k, spot, side], device)
+            if k != Z_FIRST:
+                for side, device in enumerate((inside, outside)):
+                    piece = part(k, owner, core, side)
+                    send(piece, piece, z_sem.at[k, spot, side], device)
             send(block, block, core_sem.at[k, spot], sibling)
 
     def pass_z(k):
@@ -297,6 +300,9 @@
             for side in range(2):
                 piece = part(k, owner, core, side)
                 arrived(piece, z_sem.at[k, spot, side])
+                if k == Z_FIRST and spot == 3:
+                    for onward in (1, 0, 2):
+                        send(piece, piece, z_sem.at[k, onward, side], (me, others[onward]))
                 send(piece, piece, core_sem.at[k, 3 + 2 * spot + side], sibling)
 
     def complete(k):
@@ -393,6 +399,7 @@
     hot = jnp.where(wanted == bucket_ref[...], 1.0, 0.0).astype(BF)
     bias_rows = contract(landing[...].reshape(128, 128), hot, ((0,), (0,)))[:16]
     build_tiles(bias_rows, matmul(bias_rows.astype(BF), strip_hot()), tile_ref)
+    exits.append(bring(tile_ref, tile_result, local_sem.at[8]))
     kv_across(self_out_ref, self_sem)
     pass_x(2)
     send_own(4)
@@ -517,13 +524,21 @@
             else:
                 wide_inner[:, :, cut] = part[:, :48]
                 wide_outer[:, :, cut] = part[:, 48:]
+        if group:
+            exits.append(bring(wide_mine, wide_mine_out, local_sem.at[9]))
+        else:
+            exits.append(bring(wide_inner, wide_inner_out, local_sem.at[10]))
+            exits.append(bring(wide_outer, wide_outer_out, local_sem.at[11]))
         left = turned_hidden[owners].reshape(4 * FF // 8, 2 * TOK)
         part = matmul(left, feed_right[:, FF:]).astype(BF).reshape(4, FF // 8, half)
         if group:
             tall_mine[...] = part
+            exits.append(bring(tall_mine, tall_mine_out, local_sem.at[12]))
         else:
             tall_inner[...] = part[:, :128]
             tall_outer[...] = part[:, 128:]
+            exits.append(bring(tall_inner, tall_inner_out, local_sem.at[13]))
+            exits.append(bring(tall_outer, tall_outer_out, local_sem.at[14]))
     for copy in sends + swaps:
         copy.wait_send()
     for copy in exits:
@@ -570,7 +585,13 @@
             jax.ShapeDtypeStruct((N_CTX, 2, ENC, D), BF),
         ],
         in_specs=[anywhere] * 12 + [inside] * 4 + [scalars],
-        out_specs=[anywhere] * 3 + [inside] * 22 + [scalars] * 2 + [anywhere] * 2,
+        out_specs=[anywhere] * 3
+        + [inside] * 3
+        + [anywhere]
+        + [inside] * 12
+        + [anywhere] * 6
+        + [scalars] * 2
+        + [anywhere] * 2,
         scratch_shapes=[pltpu.VMEM(pack, BF) for pack in packs]
         + [
             pltpu.VMEM((N_CTX, 2, TOK, D), BF),
@@ -585,6 +606,13 @@
             pltpu.VMEM((2, TOK, FF), BF),
             pltpu.VMEM((8, 96, 2 * TOK), BF),
             pltpu.VMEM((8, FF // 8, 2 * TOK), BF),
+            pltpu.VMEM((HEADS, 5, HALF, TOK), F32),
+            pltpu.VMEM((4, 96, FF), BF),
+            pltpu.VMEM((4, 48, FF), BF),
+            pltpu.VMEM((4, 48, FF), BF),
+            pltpu.VMEM((4, 256, D // 2), BF),
+            pltpu.VMEM((4, 128, D // 2), BF),
+            pltpu.VMEM((4, 128, D // 2), BF),
             dma((5 * 22 + 7 + 2 * 18,)),
             dma((5, 3)),
             dma((5, 4, 2)),
@@ -594,7 +622,7 @@
             dma((N_CTX, 2)),
             dma((N_CTX, 2)),
             dma((2, 3)),
-            dma((8,)),
+            dma((15,)),
         ],
         compiler_params=pltpu.CompilerParams(
             collective_id=collective_id, has_side_effects=True, vmem_limit_bytes=60 * MIB
@@ -618,7 +646,7 @@
     rights = refs[4:8]
     wide_refs, down_refs = refs[8:11], refs[11:14]
     dkv_ref, dckv_ref, square_ref = refs[14:17]
-    state_ref, kv_ref, ckv_ref, dq_ref, dmid_ref, token_ref, gain_ref, small_ref = refs[17:25]
+    kv_source, ckv_source, state_ref, dq_ref, dmid_ref, token_ref, gain_ref, small_ref = refs[17:25]
     early_out, late_out, small_out, decoder_ref, encoder_ref = refs[25:30]
     (
         left_all, right_all, turned, turned_one, turned_state, state_all, s_right, c_right,
@@ -627,7 +655,7 @@
         c_kept, c_core, c_row, c_via, c_stage, c_high, c_fin,
         small_f32, sm_own, sm_core, sm_z, sm_x, sm_ctx, sm_total,
         packed, from_ctx, land, late_packed, late_from, late_land,
-        wide_add, down_add, query_ref, bring_sem,
+        wide_add, down_add, query_ref, kv_ref, ckv_ref, bring_sem,
         s_sem, c_sem, fill_sem, act_send, act_recv, late_send, late_recv, z_send, z_recv,
         x_send, x_recv, ctx_send, ctx_recv, pass_send, pass_recv, sm_send, sm_recv, local_sem,
     ) = refs[30:]
@@ -941,6 +969,8 @@
     state_far = go(
         state_ref, state_all.at[pl.ds(ENC, ENC)], late_send.at[2], late_recv.at[2], sibling
     )
+    kv_copy = bring(kv_source, kv_ref, bring_sem.at[7])
+    ckv_copy = bring(ckv_source, ckv_ref, bring_sem.at[8])
     query_copy = bring(square_ref.at[:, :, pl.ds(0, D)], query_ref, bring_sem.at[6])
     for copy in down_copies:
         copy.wait()
@@ -961,31 +991,33 @@
     make(1)
     s_onward = rows_via(s_state, s_kept, s_via, s_row, s_sem)
     c_state = rows_send(c_copies, c_kept, c_core, c_via, c_row, c_sem)
-    make(2)
-    make(3)
     step_via(DOWN)
     step_via(WIDE)
-    for k in range(4):
-        step_z(k)
     state_near.wait()
     state_far.wait_recv()
     turned_state[...] = state_all[...].T.reshape(8, PIECE, 2 * ENC)
     s_last = rows_across(s_onward, s_kept, s_row, s_stage, s_high, s_sem)
+    make(2)
+    make(3)
     c_onward = rows_via(c_state, c_kept, c_via, c_row, c_sem)
-    for k in range(4):
-        step_via(k)
+    step_z(0)
+    step_z(1)
+    s_far = rows_sum(s_last, s_kept, s_row, s_high, s_fin, s_right, 0)
     step_x(DOWN)
-    step_x(WIDE)
-    s_far = rows_sum(s_last, s_kept, s_row, s_high, s_fin, s_right, 0)
-    for k in range(4):
-        step_x(k)
-    early = ctx_start(0, packed, from_ctx)
     s_far.wait_recv()
     multiply(SELF_KV, turned_one, s_right[...])
+    step_z(2)
+    step_z(3)
+    step_via(0)
+    step_via(1)
+    step_x(WIDE)
     c_last = rows_across(c_onward, c_kept, c_row, c_stage, c_high, c_sem)
+    step_via(2)
+    step_via(3)
     tokens = token_ref[...].astype(F32)
     d_kv = jnp.concatenate([s_fin[0], s_fin[1]], axis=1)
     query_copy.wait()
+    kv_copy.wait()
     grad = contract(dq_ref[...], query_ref[...].reshape(D, D), ((1,), (1,)))
     grad = grad + contract(d_kv, kv_ref[...], ((1,), (1,)))
     inverse = lax.rsqrt(jnp.mean(tokens * tokens, axis=-1, keepdims=True) + 1e-06)
@@ -996,6 +1028,9 @@
     sm_own[...] = small_f32[...].astype(BF)
     sm_over = go(sm_own, sm_core, sm_send.at[0], sm_recv.at[0], sibling)
     c_far = rows_sum(c_last, c_kept, c_row, c_high, c_fin, c_right, 1)
+    for k in range(4):
+        step_x(k)
+    early = ctx_start(0, packed, from_ctx)
     c_far.wait_recv()
     multiply(CROSS_KV, turned_state, c_right[...])
     step_z(SELF_KV)
@@ -1040,6 +1075,7 @@
     ctx_pass(0, land)
     ctx_sum(1, late, late_packed, late_from, late_land)
     d_ckv = jnp.concatenate([c_fin[0], c_fin[1]], axis=1)
+    ckv_copy.wait()
     encoder_ref[...] = contract(d_ckv, ckv_ref[...], ((1,), (1,)))
     sm_sum = sm_total[...].astype(F32)
     for spot in range(7):
@@ -1047,18 +1083,22 @@
         sm_sum = sm_sum + sm_ctx[spot].astype(F32)
     small_out[...] = sm_sum
     ctx_done(0, land)
-    early_out[...] = land[...]
+    early_exit = bring(land, early_out, bring_sem.at[9])
     ctx_pass(1, late_land)
     ctx_done(1, late_land)
-    late_out[...] = late_land[...]
+    late_exit = bring(late_land, late_out, bring_sem.at[10])
+    early_exit.wait()
+    late_exit.wait()
     for copy in sends:
         if copy is not sm_over:
             copy.wait_send()
 
 
 def unpack_kernel(early, late, *refs):
-    square_refs = refs[:8]
-    gate_ref, up_ref, down_ref = refs[8:]
+    for source, target in zip(refs[:3], refs[14:]):
+        target[...] = source[...]
+    square_refs = refs[3:11]
+    gate_ref, up_ref, down_ref = refs[11:14]
     half = D // 2
     middle = PIECE // 2
     for side in range(2):
@@ -1082,20 +1122,21 @@
                 ] = early[piece, side, part * 32 : part * 32 + 32, 256:].astype(F32)
 
 
-def unpack(early, late):
+def unpack(early, late, *whole):
     outs = (
         [jax.ShapeDtypeStruct((PIECE, D), F32)] * 8
         + [jax.ShapeDtypeStruct((PIECE, FF), F32)] * 2
         + [jax.ShapeDtypeStruct((FF // 8, D), F32)]
+        + [jax.ShapeDtypeStruct(part.shape, F32) for part in whole]
     )
     return pl.pallas_call(
         unpack_kernel,
         out_shape=outs,
-        in_specs=[pl.BlockSpec(memory_space=pltpu.VMEM)] * 2,
+        in_specs=[pl.BlockSpec(memory_space=pltpu.VMEM)] * (2 + len(whole)),
         out_specs=[pl.BlockSpec(memory_space=pltpu.VMEM)] * len(outs),
         compiler_params=pltpu.CompilerParams(vmem_limit_bytes=24 * MIB),
         name="unpack",
-    )(early, late)
+    )(early, late, *whole)
 
 
 def finish(far, near, collective_id):
@@ -1124,7 +1165,8 @@
         out_shape=outs,
         in_specs=[pl.BlockSpec(memory_space=pl.ANY)] * len(far)
         + [pl.BlockSpec(memory_space=pltpu.VMEM)] * len(near),
-        out_specs=[pl.BlockSpec(memory_space=pltpu.VMEM)] * len(outs),
+        out_specs=[pl.BlockSpec(memory_space=pl.ANY)] * 2
+        + [pl.BlockSpec(memory_space=pltpu.VMEM)] * 3,
         scratch_shapes=[
             pltpu.VMEM((2 * TOK, sum(LEFT)), BF),
             pltpu.VMEM((2 * TOK, sum(RIGHT)), BF),
@@ -1161,7 +1203,9 @@
             pltpu.VMEM((2, 4, PIECE // 2, FF), BF),
             pltpu.VMEM((2, 4, FF // 16, D // 2), BF),
             pltpu.VMEM((8, PIECE, D), BF),
-            dma((7,)),
+            pltpu.VMEM((D, 2 * D), BF),
+            pltpu.VMEM((D, 2 * D), BF),
+            dma((11,)),
             dma((5, 7)),
             dma((5, 7)),
             dma((4, 2)),
@@ -1442,11 +1486,11 @@
             d_kv_all.reshape(8, 2, 2, TOK, D),
             d_cross_kv_all.reshape(8, 2, 2, ENC, D),
             square,
+            kv_one,
+            kv_two,
         ],
         [
             states,
-            kv_one,
-            kv_two,
             d_queries,
             d_mid_one,
             decoder_in[0],
@@ -1459,8 +1503,8 @@
     (
         grad_out_two, grad_query_two, grad_out_one, grad_query_one,
         grad_key_two, grad_value_two, grad_key_one, grad_value_one,
-        grad_gate, grad_up, grad_down,
-    ) = unpack(early, late)
+        grad_gate, grad_up, grad_down, block_out, grad_decoder, grad_encoder,
+    ) = unpack(early, late, block_out, grad_decoder, grad_encoder)
     return (
         block_out[None],
         grad_decoder[None],

time: 280 us -> 290 us (1.036)
  Pallas kernels: 242 us -> 253 us
    pallas_call x1, Pallas kernels: 104 us -> 112 us  [front(): pl.pallas_call(front_kernel, out_shape=[jax.ShapeDtypeStruct(pack, BF) fo...]
    unnamed x49 -> x46, local copies, waits for them, and re-layouts: 9.6 us -> 9.34 us
  transfers between devices with their start and end apart: 4 -> 4, of which waited for: 2 -> 2; matrix products, arithmetic and copies ran while one was open for 4% -> 4% of each run, Pallas kernels for 8% -> 7%
where the time goes in v1:
time: 290 us; the launch traced here: 289 us
  Pallas kernels  253 us (87%)
  local copies, waits for them, and re-layouts  13.9 us (5%)
  other arithmetic  7.43 us (3%)
  matrix products  6.86 us (2%)
  starting transfers between devices  3.61 us (1%)
  waiting for transfers between devices  3.57 us (1%)
    pallas_call x1, Pallas kernels, finish(): pl.pallas_call(finish_kernel, out_shape=outs, in_specs=[pl.BlockSpec(memo...  116 us
    pallas_call x1, Pallas kernels, front(): pl.pallas_call(front_kernel, out_shape=[jax.ShapeDtypeStruct(pack, BF) fo...  112 us
    pallas_call x2, Pallas kernels, attend_back(): pl.pallas_call(functools.partial(backward_kernel, biased), grid=(PAIRS,),...  21.7 us
    unnamed x46, local copies, waits for them, and re-layouts  9.34 us
    dot_general x4, matrix products, contract(): lax.dot_general(left, right, (dims, ((), ())), preferred_element_type=F32)  6.6 us
  transfers between devices with their start and end apart: 4, of which 2 were waited for; matrix products, arithmetic and copies ran while one was open for 4% of the time, Pallas kernels for 7%

profile of v1, /device:TPU:1, one launch (start us, length us, event | category | flops | bytes accessed | tf_op | source)
XLA Modules:
  0.0 289.3 jit_solution(9138832017798857189)
XLA Ops:
  0.7 0.7 fusion.37
  1.4 1.3 fusion.32.refs_11_
  2.6 112.4 %front.1 = (bf16[8,96,1536]{2,1,0:T(8,128)(2,1)}, bf16[8,96,1536]{2,1,0:T(8,128)(2,1)}, bf16[8,96,3072]{2,1,0:T(8,128)(2,1)}, f32[3,768]{1,0:T(4,128)}, bf16[128...) custom-call(bf16[96,768]{1,0:T(8,128)(2,1)} %refs_0_.1, ...), custom_call_target="tpu_custom_call" | custom-call | tf_op jit(solution)/shard_map/front/pallas_call | solution.py:556
  115.7 0.8 collective-permute-start.2
  116.6 2.1 collective-permute-start.3
  118.7 1.1 multiply_reduce_fusion.2
  119.8 1.4 fusion.42
  121.2 0.9 copy-done.9
  122.1 0.9 copy-done.10
  123.1 0.8 copy-done.13
  123.9 8.3 %attend_cross_back.1 = (bf16[128,768]{1,0:T(8,128)(2,1)S(1)}, bf16[16,2,64,768]{3,2,1,0:T(8,128)(2,1)S(1)}) custom-call(bf16[128,768]{1,0:T(8,128)(2,1)S(1)} %copy-done.9, bf16[16,2,64,768]{3,2,1,0:T(8,128)(2,1)} %get-tuple-element.90.refs_1_.refs_2_, bf16[16,2,64,768]{3,2,1,0:T(8,128)(2,1)} %get-tuple-element.90.refs_1_.refs_2_, ...), custom_call_target="tpu_custom_call" | custom-call | flops 1000 | bytes 1000 | tf_op jit(solution)/shard_map/attend_cross_back/pallas_call | solution.py:1321
  132.2 2.9 %multiply_reduce_fusion = (f32[768]{0:T(1024)S(1)}, f32[128]{0:T(128)S(1)}, f32[128,768]{1,0:T(8,128)S(1)}) fusion(f32[128,768]{1,0:T(8,128)S(1)} %copy-done.17, f32[128]{0:T(128)S(1)} %add_rsqrt_fusion, f32[768]{0:T(1024)S(1)} %get-tuple-element.157, bf16[128,768]{1,0:T(8,128)(2,1)S(1)} %get-tuple-element.93.refs_5_, bf16[768,3072]{1,0:T(8,128)(2,1)} %bitcast.35), kind=kOutput, calls=%fused_computation.17 | convolution fusion | flops 151583872 | bytes 2169856 | tf_op jit(solution)/shard_map/dot_general | solution.py:52
  135.2 2.2 fusion.2
  137.3 0.9 fusion.41
  138.5 1.8 fusion.8.refs_5_
  140.3 2.3 collective-permute-done.2.refs_12_
  142.5 1.3 collective-permute-done.3.refs_13_
  143.9 13.4 %attend_self_back.1 = (bf16[128,768]{1,0:T(8,128)(2,1)S(1)}, bf16[16,2,128,768]{3,2,1,0:T(8,128)(2,1)}, f32[12,3,64,128]{3,2,1,0:T(8,128)S(1)}) custom-call(s32[2,32]{1,0:T(2,128)S(1)} %copy-done.14, s32[2,3]{1,0:T(2,128)S(1)} %copy-done.15, bf16[128,768]{1,0:T(8,128)(2,1)S(1)} %copy-done.8, bf16[16,2,128,768]{3,2,1,0:T(8,128)(2,1)} %get-tuple-element.110.refs_3_.refs_4_, ...), custom_call_target="tpu_custom_call" | custom-call | flops 1000 | bytes 1000 | tf_op jit(solution)/shard_map/attend_self_back/pallas_call | solution.py:1321
  157.3 0.7 copy-done.3
  158.0 0.9 copy-done.19
  159.6 0.6 copy-done.16
  160.2 0.9 fusion.11
  161.2 0.9 fusion.13
  162.6 0.7 select_maximum_fusion.refs_24_
  163.3 116.3 %finish_gradients.1 = (bf16[8,2,144,384]{3,2,1,0:T(8,128)(2,1)}, bf16[8,2,48,384]{3,2,1,0:T(8,128)(2,1)}, f32[16,128]{1,0:T(8,128)}, f32[128,768]{1,0:T(8,128)}, f32[64,768]{1,0:T(8,128)}) custom-call(bf16[128,768]{1,0:T(8,128)(2,1)} %get-tuple-element.84.refs_0_, bf16[128,768]{1,0:T(8,128)(2,1)} %get-tuple-element.85.refs_1_, ...), custom_call_target="tpu_custom_call" | custom-call | tf_op jit(solution)/shard_map/finish_gradients/pallas_call | solution.py:1163
  279.6 1.3 slice_bitcast_fusion
  280.9 1.2 slice.42
  282.1 1.5 copy-done.2
  283.6 1.1 copy-done.4
  284.6 1.0 copy-done.6
  285.6 0.9 copy-done.11
  286.6 2.7 unpack.1
  (58 shorter events, 2.3 us)
Async XLA Ops:
  115.0 42.9 %collective-permute-start = (bf16[4,48,2048]{2,1,0:T(8,128)(2,1)}, bf16[4,48,2048]{2,1,0:T(8,128)(2,1)S(1)}, u32[]{:S(2)}, u32[]{:S(2)}) collective-permute-start(bf16[4,48,2048]{2,1,0:T(8,128)(2,1)} %get-tuple-element.99), channel_id=1, source_target_pairs={{0,4},{1,5},{2,6},{3,7},{4,0},{5,1},{6,2},{7,3},{8,12},{9,13},{10,... | collective-permute-start | bytes 2359304 | tf_op jit(solution)/shard_map/ppermute | solution.py:1390
  115.1 42.8 %collective-permute-start.1 = (bf16[4,48,2048]{2,1,0:T(8,128)(2,1)}, bf16[4,48,2048]{2,1,0:T(8,128)(2,1)}, u32[]{:S(2)}, u32[]{:S(2)}) collective-permute-start(bf16[4,48,2048]{2,1,0:T(8,128)(2,1)} %get-tuple-element.100), channel_id=1, source_target_pairs={{0,20},{1,21},{2,22},{3,23},{4,16},{5,17},{6,18},{7,19},{8,28},{9,... | collective-permute-start | bytes 2359304 | tf_op jit(solution)/shard_map/ppermute | solution.py:1390
  115.7 26.8 %collective-permute-start.2 = (bf16[4,128,384]{2,1,0:T(8,128)(2,1)}, bf16[4,128,384]{2,1,0:T(8,128)(2,1)}, u32[]{:S(2)}, u32[]{:S(2)}) collective-permute-start(bf16[4,128,384]{2,1,0:T(8,128)(2,1)} %get-tuple-element.102), channel_id=1, source_target_pairs={{0,4},{1,5},{2,6},{3,7},{4,0},{5,1},{6,2},{7,3},{8,12},{9,13},{10,... | collective-permute-start | bytes 1179656 | tf_op jit(solution)/shard_map/ppermute | solution.py:1390
  116.6 27.3 %collective-permute-start.3 = (bf16[4,128,384]{2,1,0:T(8,128)(2,1)}, bf16[4,128,384]{2,1,0:T(8,128)(2,1)}, u32[]{:S(2)}, u32[]{:S(2)}) collective-permute-start(bf16[4,128,384]{2,1,0:T(8,128)(2,1)} %get-tuple-element.103), channel_id=1, source_target_pairs={{0,20},{1,21},{2,22},{3,23},{4,16},{5,17},{6,18},{7,19},{8,28},{9,... | collective-permute-start | bytes 1179656 | tf_op jit(solution)/shard_map/ppermute | solution.py:1390
  121.2 0.9 copy-start.9
  122.1 0.9 copy-start.10
  123.1 0.8 copy-start.13
  123.9 8.3 %copy-start.17 = (f32[128,768]{1,0:T(8,128)S(1)}, f32[128,768]{1,0:T(8,128)}, u32[]{:S(2)}) copy-start(f32[128,768]{1,0:T(8,128)} %get-tuple-element.95) | copy-start | bytes 1179652
  132.1 6.1 %copy-start = (bf16[16,2,64,768]{3,2,1,0:T(8,128)(2,1)}, bf16[16,2,64,768]{3,2,1,0:T(8,128)(2,1)S(1)}, u32[]{:S(2)}) copy-start(bf16[16,2,64,768]{3,2,1,0:T(8,128)(2,1)S(1)} %get-tuple-element.125) | copy-start | bytes 9437188
  132.1 6.1 %copy-start.7 = (bf16[128,768]{1,0:T(8,128)(2,1)}, bf16[128,768]{1,0:T(8,128)(2,1)S(1)}, u32[]{:S(2)}) copy-start(bf16[128,768]{1,0:T(8,128)(2,1)S(1)} %get-tuple-element.93.refs_5_) | copy-start | bytes 589828
  132.2 5.2 %copy-start.20 = (f32[128,768]{1,0:T(8,128)S(1)}, f32[128,768]{1,0:T(8,128)}, u32[]{:S(2)}) copy-start(f32[128,768]{1,0:T(8,128)} %get-tuple-element.94) | copy-start | bytes 1179652
  135.1 3.1 %copy-start.21 = (f32[1,768]{1,0:T(1,128)S(1)}, f32[1,768]{1,0:T(1,128)}, u32[]{:S(2)}) copy-start(f32[1,768]{1,0:T(1,128)} %get-tuple-element.128) | copy-start | bytes 9220
  135.1 8.7 %copy-start.1 = (f32[12,5,64,128]{3,2,1,0:T(8,128)S(1)}, f32[12,5,64,128]{3,2,1,0:T(8,128)}, u32[]{:S(2)}) copy-start(f32[12,5,64,128]{3,2,1,0:T(8,128)} %get-tuple-element.113.refs_7_) | copy-start | bytes 5898244
  135.1 8.7 %copy-start.8 = (bf16[128,768]{1,0:T(8,128)(2,1)S(1)}, bf16[128,768]{1,0:T(8,128)(2,1)}, u32[]{:S(2)}) copy-start(bf16[128,768]{1,0:T(8,128)(2,1)} %get-tuple-element.109.refs_2_) | copy-start | bytes 589828
  135.1 8.7 %copy-start.12 = (f32[6,8,256]{2,1,0:T(8,128)S(1)}, f32[6,8,256]{2,1,0:T(8,128)}, u32[]{:S(2)}) copy-start(f32[6,8,256]{2,1,0:T(8,128)} %get-tuple-element.112.refs_6_) | copy-start | bytes 147460
  135.2 8.7 %copy-start.14 = (s32[2,32]{1,0:T(2,128)S(1)}, s32[2,32]{1,0:T(2,128)}, u32[]{:S(2)}) copy-start(s32[2,32]{1,0:T(2,128)} %get-tuple-element.107.refs_0_) | copy-start | bytes 772
  135.2 8.7 %copy-start.15 = (s32[2,3]{1,0:T(2,128)S(1)}, s32[2,3]{1,0:T(2,128)}, u32[]{:S(2)}) copy-start(s32[2,3]{1,0:T(2,128)} %get-tuple-element.108.refs_1_) | copy-start | bytes 76
  138.2 19.0 %copy-start.18 = (bf16[128,768]{1,0:T(8,128)(2,1)}, bf16[128,768]{1,0:T(8,128)(2,1)S(1)}, u32[]{:S(2)}) copy-start(bf16[128,768]{1,0:T(8,128)(2,1)S(1)} %get-tuple-element.154.refs_6_) | copy-start | bytes 589828
  157.3 0.7 copy-start.3
  157.9 0.9 copy-start.19
  158.8 1.4 copy-start.16
  160.2 2.1 copy-start.22
  163.3 118.8 %copy-start.5 = (f32[128,768]{1,0:T(8,128)S(1)}, f32[128,768]{1,0:T(8,128)}, u32[]{:S(2)}) copy-start(f32[128,768]{1,0:T(8,128)} %get-tuple-element.132.refs_0_) | copy-start | bytes 1179652
  282.1 1.5 copy-start.2
  283.6 1.1 copy-start.4
  284.6 1.0 copy-start.6
  285.6 0.9 copy-start.11

commit v2 on v1

--- a/solution.py
+++ b/solution.py
@@ -195,7 +195,6 @@
     pl.semaphore_wait(barrier, len(devices))
 
 
-Z_FIRST = 4
 ROOT = (2.0 / 3.141592653589793) ** 0.5
 PACKS = ((0, 1), (2, 3), (4, 5, 6, 7), (8, 9), (10,))
 
@@ -288,10 +287,9 @@
             owner = low * 4 + (x + 3 - spot) % 4
             block = part(k, owner, core)
             arrived(block, x_sem.at[k, spot])
-            if k != Z_FIRST:
-                for side, device in enumerate((inside, outside)):
-                    piece = part(k, owner, core, side)
-                    send(piece, piece, z_sem.at[k, spot, side], device)
+            for side, device in enumerate((inside, outside)):
+                piece = part(k, owner, core, side)
+                send(piece, piece, z_sem.at[k, spot, side], device)
             send(block, block, core_sem.at[k, spot], sibling)
 
     def pass_z(k):
@@ -300,9 +298,6 @@
             for side in range(2):
                 piece = part(k, owner, core, side)
                 arrived(piece, z_sem.at[k, spot, side])
-                if k == Z_FIRST and spot == 3:
-                    for onward in (1, 0, 2):
-                        send(piece, piece, z_sem.at[k, onward, side], (me, others[onward]))
                 send(piece, piece, core_sem.at[k, 3 + 2 * spot + side], sibling)
 
     def complete(k):
@@ -385,6 +380,7 @@
     kv_start(self_ref, self_out_ref, self_sem)
     own_self = bring(self_ref, self_out_ref.at[me], local_sem.at[2])
     pass_z(1)
+    send_own(4)
     complete(1)
     exits.append(bring(targets[1], results[1], local_sem.at[4]))
     for half in range(2):
@@ -402,7 +398,6 @@
     exits.append(bring(tile_ref, tile_result, local_sem.at[8]))
     kv_across(self_out_ref, self_sem)
     pass_x(2)
-    send_own(4)
     kv_near(self_out_ref, self_sem, False)
     pass_z(2)
     kv_across(cross_out_ref, cross_sem)
@@ -448,13 +443,12 @@
     normed_two = rms_scaled(mid_one, gain[1])
     normed_two_ref[...] = normed_two
     cross_query_ref[...] = matmul(normed_two, square(2)).astype(BF)
-    pass_z(4)
     kv_complete(cross_out_ref, cross_sem)
     exits.append(bring(cross_out_ref, cross_result, local_sem.at[7]))
     attend_cross(0, 3)
+    pass_z(4)
+    attend_cross(3, 6)
     complete(3)
-    attend_cross(3, 6)
-    complete(4)
     mid_two = mid_one_ref[...] + matmul(cross_attended_ref[...], square(3))
 
 
@@ -474,12 +468,17 @@
         steep = 0.5 * (1.0 + curve) + 0.5 * gate * (1.0 - curve * curve) * (
             ROOT * (1.0 + 3.0 * 0.044715 * square_gate)
         )
-        d_hidden = contract(
-            upstream, targets[4][2 * piece : 2 * piece + 2].reshape(512, D), ((1,), (1,))
-        )
         feed_left[near_rows, D + start : D + start + 512] = (raised * up).astype(BF)
-        slope_ref[0, :, start : start + 512] = (d_hidden * up * steep).astype(BF)
-        slope_ref[1, :, start : start + 512] = (d_hidden * raised).astype(BF)
+        for side in range(2):
+            cut = slice(side * 256, side * 256 + 256)
+            score_ref[2 * piece + side] = (up * steep)[:, cut]
+            score_ref[8 + 2 * piece + side] = raised[:, cut]
+    complete(4)
+    for piece in range(8):
+        start = piece * 256
+        d_hidden = contract(upstream, targets[4][piece], ((1,), (1,)))
+        slope_ref[0, :, start : start + 256] = (d_hidden * score_ref[piece]).astype(BF)
+        slope_ref[1, :, start : start + 256] = (d_hidden * score_ref[8 + piece]).astype(BF)
     half = D // 2
     near_half = pl.ds(pl.multiple_of(core * half, 128), half)
     far_half = pl.ds(pl.multiple_of((1 - core) * half, 128), half)
@@ -991,29 +990,28 @@
     make(1)
     s_onward = rows_via(s_state, s_kept, s_via, s_row, s_sem)
     c_state = rows_send(c_copies, c_kept, c_core, c_via, c_row, c_sem)
+    make(2)
+    make(3)
     step_via(DOWN)
     step_via(WIDE)
+    for k in range(4):
+        step_z(k)
     state_near.wait()
     state_far.wait_recv()
     turned_state[...] = state_all[...].T.reshape(8, PIECE, 2 * ENC)
     s_last = rows_across(s_onward, s_kept, s_row, s_stage, s_high, s_sem)
-    make(2)
-    make(3)
     c_onward = rows_via(c_state, c_kept, c_via, c_row, c_sem)
-    step_z(0)
-    step_z(1)
+    for k in range(4):
+        step_via(k)
+    step_x(DOWN)
+    step_x(WIDE)
     s_far = rows_sum(s_last, s_kept, s_row, s_high, s_fin, s_right, 0)
-    step_x(DOWN)
+    for k in range(4):
+        step_x(k)
+    early = ctx_start(0, packed, from_ctx)
     s_far.wait_recv()
     multiply(SELF_KV, turned_one, s_right[...])
-    step_z(2)
-    step_z(3)
-    step_via(0)
-    step_via(1)
-    step_x(WIDE)
     c_last = rows_across(c_onward, c_kept, c_row, c_stage, c_high, c_sem)
-    step_via(2)
-    step_via(3)
     tokens = token_ref[...].astype(F32)
     d_kv = jnp.concatenate([s_fin[0], s_fin[1]], axis=1)
     query_copy.wait()
@@ -1028,9 +1026,6 @@
     sm_own[...] = small_f32[...].astype(BF)
     sm_over = go(sm_own, sm_core, sm_send.at[0], sm_recv.at[0], sibling)
     c_far = rows_sum(c_last, c_kept, c_row, c_high, c_fin, c_right, 1)
-    for k in range(4):
-        step_x(k)
-    early = ctx_start(0, packed, from_ctx)
     c_far.wait_recv()
     multiply(CROSS_KV, turned_state, c_right[...])
     step_z(SELF_KV)

time: 290 us -> 279 us (0.962)
  Pallas kernels: 253 us -> 242 us
    pallas_call x1, Pallas kernels: 112 us -> 104 us  [front(): pl.pallas_call(front_kernel, out_shape=[jax.ShapeDtypeStruct(pack, BF) fo...]
  transfers between devices with their start and end apart: 4 -> 4, of which waited for: 2 -> 2; matrix products, arithmetic and copies ran while one was open for 4% -> 4% of each run, Pallas kernels for 7% -> 8%
where the time goes in v2:
time: 279 us; the launch traced here: 278 us
  Pallas kernels  242 us (87%)
  local copies, waits for them, and re-layouts  13.9 us (5%)
  other arithmetic  7.43 us (3%)
  matrix products  6.86 us (2%)
  waiting for transfers between devices  3.99 us (1%)
  starting transfers between devices  3.62 us (1%)
    pallas_call x1, Pallas kernels, finish(): pl.pallas_call(finish_kernel, out_shape=outs, in_specs=[pl.BlockSpec(memo...  114 us
    pallas_call x1, Pallas kernels, front(): pl.pallas_call(front_kernel, out_shape=[jax.ShapeDtypeStruct(pack, BF) fo...  104 us
    pallas_call x2, Pallas kernels, attend_back(): pl.pallas_call(functools.partial(backward_kernel, biased), grid=(PAIRS,),...  21.7 us
    unnamed x46, local copies, waits for them, and re-layouts  9.34 us
    dot_general x4, matrix products, contract(): lax.dot_general(left, right, (dims, ((), ())), preferred_element_type=F32)  6.6 us
  transfers between devices with their start and end apart: 4, of which 2 were waited for; matrix products, arithmetic and copies ran while one was open for 4% of the time, Pallas kernels for 8%

profile of v2, /device:TPU:1, one launch (start us, length us, event | category | flops | bytes accessed | tf_op | source)
XLA Modules:
  0.0 278.4 jit_solution(944473595530815293)
XLA Ops:
  0.7 0.7 fusion.37
  1.4 1.3 fusion.32.refs_11_
  2.6 103.7 %front.1 = (bf16[8,96,1536]{2,1,0:T(8,128)(2,1)}, bf16[8,96,1536]{2,1,0:T(8,128)(2,1)}, bf16[8,96,3072]{2,1,0:T(8,128)(2,1)}, f32[3,768]{1,0:T(4,128)}, bf16[128...) custom-call(bf16[96,768]{1,0:T(8,128)(2,1)} %refs_0_.1, ...), custom_call_target="tpu_custom_call" | custom-call | tf_op jit(solution)/shard_map/front/pallas_call | solution.py:555
  106.7 0.9 collective-permute-start.1
  108.1 1.9 collective-permute-start.3
  110.0 1.1 multiply_reduce_fusion.2
  111.1 1.4 fusion.42
  112.5 0.9 copy-done.9
  113.4 0.9 copy-done.10
  114.4 0.8 copy-done.13
  115.2 8.3 %attend_cross_back.1 = (bf16[128,768]{1,0:T(8,128)(2,1)S(1)}, bf16[16,2,64,768]{3,2,1,0:T(8,128)(2,1)S(1)}) custom-call(bf16[128,768]{1,0:T(8,128)(2,1)S(1)} %copy-done.9, bf16[16,2,64,768]{3,2,1,0:T(8,128)(2,1)} %get-tuple-element.90.refs_1_.refs_2_, bf16[16,2,64,768]{3,2,1,0:T(8,128)(2,1)} %get-tuple-element.90.refs_1_.refs_2_, ...), custom_call_target="tpu_custom_call" | custom-call | flops 1000 | bytes 1000 | tf_op jit(solution)/shard_map/attend_cross_back/pallas_call | solution.py:1316
  123.5 2.9 %multiply_reduce_fusion = (f32[768]{0:T(1024)S(1)}, f32[128]{0:T(128)S(1)}, f32[128,768]{1,0:T(8,128)S(1)}) fusion(f32[128,768]{1,0:T(8,128)S(1)} %copy-done.17, f32[128]{0:T(128)S(1)} %add_rsqrt_fusion, f32[768]{0:T(1024)S(1)} %get-tuple-element.157, bf16[128,768]{1,0:T(8,128)(2,1)S(1)} %get-tuple-element.93.refs_5_, bf16[768,3072]{1,0:T(8,128)(2,1)} %bitcast.35), kind=kOutput, calls=%fused_computation.17 | convolution fusion | flops 151583872 | bytes 2169856 | tf_op jit(solution)/shard_map/dot_general | solution.py:52
  126.5 2.2 fusion.2
  128.7 0.9 fusion.41
  129.8 1.8 fusion.8.refs_5_
  131.6 2.8 collective-permute-done.2.refs_12_
  134.3 1.2 collective-permute-done.3.refs_13_
  135.6 13.4 %attend_self_back.1 = (bf16[128,768]{1,0:T(8,128)(2,1)S(1)}, bf16[16,2,128,768]{3,2,1,0:T(8,128)(2,1)}, f32[12,3,64,128]{3,2,1,0:T(8,128)S(1)}) custom-call(s32[2,32]{1,0:T(2,128)S(1)} %copy-done.14, s32[2,3]{1,0:T(2,128)S(1)} %copy-done.15, bf16[128,768]{1,0:T(8,128)(2,1)S(1)} %copy-done.8, bf16[16,2,128,768]{3,2,1,0:T(8,128)(2,1)} %get-tuple-element.110.refs_3_.refs_4_, ...), custom_call_target="tpu_custom_call" | custom-call | flops 1000 | bytes 1000 | tf_op jit(solution)/shard_map/attend_self_back/pallas_call | solution.py:1316
  149.0 0.7 copy-done.3
  149.7 0.9 copy-done.19
  151.3 0.6 copy-done.16
  152.0 0.9 fusion.11
  152.9 0.9 fusion.13
  154.3 0.7 select_maximum_fusion.refs_24_
  155.0 113.7 %finish_gradients.1 = (bf16[8,2,144,384]{3,2,1,0:T(8,128)(2,1)}, bf16[8,2,48,384]{3,2,1,0:T(8,128)(2,1)}, f32[16,128]{1,0:T(8,128)}, f32[128,768]{1,0:T(8,128)}, f32[64,768]{1,0:T(8,128)}) custom-call(bf16[128,768]{1,0:T(8,128)(2,1)} %get-tuple-element.84.refs_0_, bf16[128,768]{1,0:T(8,128)(2,1)} %get-tuple-element.85.refs_1_, ...), custom_call_target="tpu_custom_call" | custom-call | tf_op jit(solution)/shard_map/finish_gradients/pallas_call | solution.py:1158
  268.7 1.3 slice_bitcast_fusion
  270.0 1.2 slice.42
  271.3 1.5 copy-done.2
  272.7 1.1 copy-done.4
  273.8 1.0 copy-done.6
  274.8 0.9 copy-done.11
  275.7 2.7 unpack.1
  (58 shorter events, 2.5 us)
Async XLA Ops:
  106.3 43.3 %collective-permute-start = (bf16[4,48,2048]{2,1,0:T(8,128)(2,1)}, bf16[4,48,2048]{2,1,0:T(8,128)(2,1)S(1)}, u32[]{:S(2)}, u32[]{:S(2)}) collective-permute-start(bf16[4,48,2048]{2,1,0:T(8,128)(2,1)} %get-tuple-element.99), channel_id=1, source_target_pairs={{0,4},{1,5},{2,6},{3,7},{4,0},{5,1},{6,2},{7,3},{8,12},{9,13},{10,... | collective-permute-start | bytes 2359304 | tf_op jit(solution)/shard_map/ppermute | solution.py:1385
  106.7 42.9 %collective-permute-start.1 = (bf16[4,48,2048]{2,1,0:T(8,128)(2,1)}, bf16[4,48,2048]{2,1,0:T(8,128)(2,1)}, u32[]{:S(2)}, u32[]{:S(2)}) collective-permute-start(bf16[4,48,2048]{2,1,0:T(8,128)(2,1)} %get-tuple-element.100), channel_id=1, source_target_pairs={{0,20},{1,21},{2,22},{3,23},{4,16},{5,17},{6,18},{7,19},{8,28},{9,... | collective-permute-start | bytes 2359304 | tf_op jit(solution)/shard_map/ppermute | solution.py:1385
  107.6 26.7 %collective-permute-start.2 = (bf16[4,128,384]{2,1,0:T(8,128)(2,1)}, bf16[4,128,384]{2,1,0:T(8,128)(2,1)}, u32[]{:S(2)}, u32[]{:S(2)}) collective-permute-start(bf16[4,128,384]{2,1,0:T(8,128)(2,1)} %get-tuple-element.102), channel_id=1, source_target_pairs={{0,4},{1,5},{2,6},{3,7},{4,0},{5,1},{6,2},{7,3},{8,12},{9,13},{10,... | collective-permute-start | bytes 1179656 | tf_op jit(solution)/shard_map/ppermute | solution.py:1385
  108.1 27.5 %collective-permute-start.3 = (bf16[4,128,384]{2,1,0:T(8,128)(2,1)}, bf16[4,128,384]{2,1,0:T(8,128)(2,1)}, u32[]{:S(2)}, u32[]{:S(2)}) collective-permute-start(bf16[4,128,384]{2,1,0:T(8,128)(2,1)} %get-tuple-element.103), channel_id=1, source_target_pairs={{0,20},{1,21},{2,22},{3,23},{4,16},{5,17},{6,18},{7,19},{8,28},{9,... | collective-permute-start | bytes 1179656 | tf_op jit(solution)/shard_map/ppermute | solution.py:1385
  112.5 0.9 copy-start.9
  113.4 0.9 copy-start.10
  114.4 0.8 copy-start.13
  115.2 8.3 %copy-start.17 = (f32[128,768]{1,0:T(8,128)S(1)}, f32[128,768]{1,0:T(8,128)}, u32[]{:S(2)}) copy-start(f32[128,768]{1,0:T(8,128)} %get-tuple-element.95) | copy-start | bytes 1179652
  123.4 6.1 %copy-start = (bf16[16,2,64,768]{3,2,1,0:T(8,128)(2,1)}, bf16[16,2,64,768]{3,2,1,0:T(8,128)(2,1)S(1)}, u32[]{:S(2)}) copy-start(bf16[16,2,64,768]{3,2,1,0:T(8,128)(2,1)S(1)} %get-tuple-element.125) | copy-start | bytes 9437188
  123.4 6.1 %copy-start.7 = (bf16[128,768]{1,0:T(8,128)(2,1)}, bf16[128,768]{1,0:T(8,128)(2,1)S(1)}, u32[]{:S(2)}) copy-start(bf16[128,768]{1,0:T(8,128)(2,1)S(1)} %get-tuple-element.93.refs_5_) | copy-start | bytes 589828
  123.5 5.2 %copy-start.20 = (f32[128,768]{1,0:T(8,128)S(1)}, f32[128,768]{1,0:T(8,128)}, u32[]{:S(2)}) copy-start(f32[128,768]{1,0:T(8,128)} %get-tuple-element.94) | copy-start | bytes 1179652
  126.4 3.1 %copy-start.21 = (f32[1,768]{1,0:T(1,128)S(1)}, f32[1,768]{1,0:T(1,128)}, u32[]{:S(2)}) copy-start(f32[1,768]{1,0:T(1,128)} %get-tuple-element.128) | copy-start | bytes 9220
  126.4 9.1 %copy-start.1 = (f32[12,5,64,128]{3,2,1,0:T(8,128)S(1)}, f32[12,5,64,128]{3,2,1,0:T(8,128)}, u32[]{:S(2)}) copy-start(f32[12,5,64,128]{3,2,1,0:T(8,128)} %get-tuple-element.113.refs_7_) | copy-start | bytes 5898244
  126.4 9.1 %copy-start.8 = (bf16[128,768]{1,0:T(8,128)(2,1)S(1)}, bf16[128,768]{1,0:T(8,128)(2,1)}, u32[]{:S(2)}) copy-start(bf16[128,768]{1,0:T(8,128)(2,1)} %get-tuple-element.109.refs_2_) | copy-start | bytes 589828
  126.5 9.1 %copy-start.12 = (f32[6,8,256]{2,1,0:T(8,128)S(1)}, f32[6,8,256]{2,1,0:T(8,128)}, u32[]{:S(2)}) copy-start(f32[6,8,256]{2,1,0:T(8,128)} %get-tuple-element.112.refs_6_) | copy-start | bytes 147460
  126.5 9.1 %copy-start.14 = (s32[2,32]{1,0:T(2,128)S(1)}, s32[2,32]{1,0:T(2,128)}, u32[]{:S(2)}) copy-start(s32[2,32]{1,0:T(2,128)} %get-tuple-element.107.refs_0_) | copy-start | bytes 772
  126.5 9.1 %copy-start.15 = (s32[2,3]{1,0:T(2,128)S(1)}, s32[2,3]{1,0:T(2,128)}, u32[]{:S(2)}) copy-start(s32[2,3]{1,0:T(2,128)} %get-tuple-element.108.refs_1_) | copy-start | bytes 76
  129.5 19.4 %copy-start.18 = (bf16[128,768]{1,0:T(8,128)(2,1)}, bf16[128,768]{1,0:T(8,128)(2,1)S(1)}, u32[]{:S(2)}) copy-start(bf16[128,768]{1,0:T(8,128)(2,1)S(1)} %get-tuple-element.154.refs_6_) | copy-start | bytes 589828
  149.0 0.7 copy-start.3
  149.7 0.9 copy-start.19
  150.5 1.4 copy-start.16
  152.0 2.1 copy-start.22
  155.0 116.2 %copy-start.5 = (f32[128,768]{1,0:T(8,128)S(1)}, f32[128,768]{1,0:T(8,128)}, u32[]{:S(2)}) copy-start(f32[128,768]{1,0:T(8,128)} %get-tuple-element.132.refs_0_) | copy-start | bytes 1179652
  271.3 1.5 copy-start.2
  272.7 1.1 copy-start.4
  273.8 1.0 copy-start.6
  274.8 0.9 copy-start.11

commit v3 on v2

--- a/solution.py
+++ b/solution.py
@@ -1129,7 +1129,7 @@
         out_shape=outs,
         in_specs=[pl.BlockSpec(memory_space=pltpu.VMEM)] * (2 + len(whole)),
         out_specs=[pl.BlockSpec(memory_space=pltpu.VMEM)] * len(outs),
-        compiler_params=pltpu.CompilerParams(vmem_limit_bytes=24 * MIB),
+        compiler_params=pltpu.CompilerParams(vmem_limit_bytes=62 * MIB),
         name="unpack",
     )(early, late, *whole)
 
@@ -1292,7 +1292,7 @@
 TILE_SPEC = pl.BlockSpec((2, 5, HALF, TOK), lambda pair: (pair, 0, 0, 0))
 TOTAL_SPEC = pl.BlockSpec((1, 8, 2 * TOK), lambda pair: (pair, 0, 0))
 ROW_SPEC = pl.BlockSpec((TOK, 2 * HEAD_DIM), pair_columns)
-LOCAL = pltpu.CompilerParams(vmem_limit_bytes=48 * MIB)
+LOCAL = pltpu.CompilerParams(vmem_limit_bytes=62 * MIB)
 
 
 def attend_back(queries, gathered, grads, totals, rows, row_block, classes=None, near=None, tiles=None):

time: 279 us -> 278 us (level)
  local copies, waits for them, and re-layouts: 13.9 us -> 6.36 us
  other arithmetic: 7.43 us -> 14.2 us
    unnamed x46 -> x16, local copies, waits for them, and re-layouts: 9.34 us -> 0.5 us
  transfers between devices with their start and end apart: 4 -> 4, of which waited for: 2 -> 2; matrix products, arithmetic and copies ran while one was open for 4% -> 5% of each run, Pallas kernels for 8% -> 8%
where the time goes in v3:
time: 278 us; the launch traced here: 277 us
  Pallas kernels  243 us (87%)
  other arithmetic  14.2 us (5%)
  matrix products  6.65 us (2%)
  local copies, waits for them, and re-layouts  6.36 us (2%)
  starting transfers between devices  3.62 us (1%)
    pallas_call x1, Pallas kernels, finish(): pl.pallas_call(finish_kernel, out_shape=outs, in_specs=[pl.BlockSpec(memo...  114 us
    pallas_call x1, Pallas kernels, front(): pl.pallas_call(front_kernel, out_shape=[jax.ShapeDtypeStruct(pack, BF) fo...  104 us
    pallas_call x2, Pallas kernels, attend_back(): pl.pallas_call(functools.partial(backward_kernel, biased), grid=(PAIRS,),...  21.9 us
    dot_general x4, matrix products, contract(): lax.dot_general(left, right, (dims, ((), ())), preferred_element_type=F32)  6.39 us
  transfers between devices with their start and end apart: 4, of which 2 were waited for; matrix products, arithmetic and copies ran while one was open for 5% of the time, Pallas kernels for 8%

profile of v3, /device:TPU:1, one launch (start us, length us, event | category | flops | bytes accessed | tf_op | source)
XLA Modules:
  0.0 276.8 jit_solution(10938217453109235094)
XLA Ops:
  0.7 0.7 fusion.37
  1.4 1.3 fusion.32.refs_11_
  2.6 103.5 %front.1 = (bf16[8,96,1536]{2,1,0:T(8,128)(2,1)}, bf16[8,96,1536]{2,1,0:T(8,128)(2,1)}, bf16[8,96,3072]{2,1,0:T(8,128)(2,1)}, f32[3,768]{1,0:T(4,128)}, bf16[128...) custom-call(bf16[96,768]{1,0:T(8,128)(2,1)} %refs_0_.1, ...), custom_call_target="tpu_custom_call" | custom-call | tf_op jit(solution)/shard_map/front/pallas_call | solution.py:555
  106.2 0.4 collective-permute-start
  106.6 0.9 collective-permute-start.1
  107.5 0.4 collective-permute-start.2
  107.9 1.9 collective-permute-start.3
  109.8 0.6 iota_shift-right-logical_fusion
  110.4 0.6 broadcast_add_fusion
  111.1 0.6 iota_shift-right-logical_fusion.1
  111.7 0.6 fusion.20
  112.3 0.6 fusion.23
  112.9 1.1 multiply_reduce_fusion.2
  114.1 1.4 fusion.42
  115.4 9.1 %attend_cross_back.1 = (bf16[128,768]{1,0:T(8,128)(2,1)}, bf16[16,2,64,768]{3,2,1,0:T(8,128)(2,1)}) custom-call(bf16[128,768]{1,0:T(8,128)(2,1)} %get-tuple-element.89.refs_0_, bf16[16,2,64,768]{3,2,1,0:T(8,128)(2,1)} %get-tuple-element.90.refs_1_.refs_2_, bf16[16,2,64,768]{3,2,1,0:T(8,128)(2,1)} %get-tuple-element.90.refs_1_.refs_2_, ...), custom_call_target="tpu_custom_call" | custom-call | flops 1000 | bytes 1000 | tf_op jit(solution)/shard_map/attend_cross_back/pallas_call | solution.py:1316
  124.5 2.1 multiply_reduce_fusion
  126.6 2.5 fusion.2
  129.1 1.5 fusion.41
  130.8 0.5 copy-done.1
  131.3 2.5 fusion.8.refs_5_
  133.8 0.4 collective-permute-done.2.refs_12_
  134.2 1.2 collective-permute-done.3.refs_13_
  135.4 12.8 %attend_self_back.1 = (bf16[128,768]{1,0:T(8,128)(2,1)}, bf16[16,2,128,768]{3,2,1,0:T(8,128)(2,1)}, f32[12,3,64,128]{3,2,1,0:T(8,128)}) custom-call(s32[2,32]{1,0:T(2,128)} %get-tuple-element.107.refs_0_, s32[2,3]{1,0:T(2,128)} %get-tuple-element.108.refs_1_, bf16[128,768]{1,0:T(8,128)(2,1)} %get-tuple-element.109.refs_2_, ...), custom_call_target="tpu_custom_call" | custom-call | flops 1000 | bytes 1000 | tf_op jit(solution)/shard_map/attend_self_back/pallas_call | solution.py:1316
  148.2 3.1 %slice_add_fusion = f32[12,3,64,64]{3,2,1,0:T(8,128)} fusion(f32[12,3,64,128]{3,2,1,0:T(8,128)} %get-tuple-element.129), kind=kLoop, calls=%fused_computation.13 | loop fusion | flops 147456 | bytes 1769472 | tf_op jit(solution)/shard_map/add | solution.py:1370
  151.4 1.7 reshape.97
  153.0 0.9 fusion.11
  154.0 0.9 fusion.13
  155.4 0.7 select_maximum_fusion.refs_24_
  156.1 113.6 %finish_gradients.1 = (bf16[8,2,144,384]{3,2,1,0:T(8,128)(2,1)}, bf16[8,2,48,384]{3,2,1,0:T(8,128)(2,1)}, f32[16,128]{1,0:T(8,128)}, f32[128,768]{1,0:T(8,128)}, f32[64,768]{1,0:T(8,128)}) custom-call(bf16[128,768]{1,0:T(8,128)(2,1)} %get-tuple-element.84.refs_0_, bf16[128,768]{1,0:T(8,128)(2,1)} %get-tuple-element.85.refs_1_, ...), custom_call_target="tpu_custom_call" | custom-call | tf_op jit(solution)/shard_map/finish_gradients/pallas_call | solution.py:1158
  269.8 1.3 slice_bitcast_fusion
  271.1 1.3 slice.42
  272.3 4.4 %unpack.1 = (f32[96,768]{1,0:T(8,128)}, f32[96,768]{1,0:T(8,128)}, f32[96,768]{1,0:T(8,128)}, f32[96,768]{1,0:T(8,128)}, f32[96,768]{1,0:T(8,128)}, /*index=5*/f...) custom-call(bf16[8,2,144,384]{3,2,1,0:T(8,128)(2,1)} %get-tuple-elem, ...), custom_call_target="tpu_custom_call" | custom-call | tf_op jit(solution)/shard_map/unpack/pallas_call | solution.py:1127
  (28 shorter events, 0.7 us)
Async XLA Ops:
  106.2 42.0 %collective-permute-start = (bf16[4,48,2048]{2,1,0:T(8,128)(2,1)}, bf16[4,48,2048]{2,1,0:T(8,128)(2,1)}, u32[]{:S(2)}, u32[]{:S(2)}) collective-permute-start(bf16[4,48,2048]{2,1,0:T(8,128)(2,1)} %get-tuple-element.99), channel_id=1, source_target_pairs={{0,4},{1,5},{2,6},{3,7},{4,0},{5,1},{6,2},{7,3},{8,12},{9,13},{10,... | collective-permute-start | bytes 2359304 | tf_op jit(solution)/shard_map/ppermute | solution.py:1385
  106.6 41.6 %collective-permute-start.1 = (bf16[4,48,2048]{2,1,0:T(8,128)(2,1)}, bf16[4,48,2048]{2,1,0:T(8,128)(2,1)}, u32[]{:S(2)}, u32[]{:S(2)}) collective-permute-start(bf16[4,48,2048]{2,1,0:T(8,128)(2,1)} %get-tuple-element.100), channel_id=1, source_target_pairs={{0,20},{1,21},{2,22},{3,23},{4,16},{5,17},{6,18},{7,19},{8,28},{9,... | collective-permute-start | bytes 2359304 | tf_op jit(solution)/shard_map/ppermute | solution.py:1385
  107.5 26.7 %collective-permute-start.2 = (bf16[4,128,384]{2,1,0:T(8,128)(2,1)}, bf16[4,128,384]{2,1,0:T(8,128)(2,1)}, u32[]{:S(2)}, u32[]{:S(2)}) collective-permute-start(bf16[4,128,384]{2,1,0:T(8,128)(2,1)} %get-tuple-element.102), channel_id=1, source_target_pairs={{0,4},{1,5},{2,6},{3,7},{4,0},{5,1},{6,2},{7,3},{8,12},{9,13},{10,... | collective-permute-start | bytes 1179656 | tf_op jit(solution)/shard_map/ppermute | solution.py:1385
  107.9 27.5 %collective-permute-start.3 = (bf16[4,128,384]{2,1,0:T(8,128)(2,1)}, bf16[4,128,384]{2,1,0:T(8,128)(2,1)}, u32[]{:S(2)}, u32[]{:S(2)}) collective-permute-start(bf16[4,128,384]{2,1,0:T(8,128)(2,1)} %get-tuple-element.103), channel_id=1, source_target_pairs={{0,20},{1,21},{2,22},{3,23},{4,16},{5,17},{6,18},{7,19},{8,28},{9,... | collective-permute-start | bytes 1179656 | tf_op jit(solution)/shard_map/ppermute | solution.py:1385
  114.0 1.4 copy-start.5
  114.0 10.5 %copy-start.4 = (f32[128]{0:T(128)}, f32[128]{0:T(128)S(1)}, u32[]{:S(2)}) copy-start(f32[128]{0:T(128)S(1)} %add_rsqrt_fusion) | copy-start | bytes 1540
  115.4 9.1 %copy-start = (f32[128,768]{1,0:T(8,128)S(1)}, f32[128,768]{1,0:T(8,128)}, u32[]{:S(2)}) copy-start(f32[128,768]{1,0:T(8,128)} %get-tuple-element.95) | copy-start | bytes 1179652
  124.5 4.6 %copy-start.6 = (f32[128]{0:T(128)S(1)}, f32[128]{0:T(128)}, u32[]{:S(2)}) copy-start(f32[128]{0:T(128)} %copy-done.5) | copy-start | bytes 1540
  124.5 4.6 %copy-start.2 = (f32[128,768]{1,0:T(8,128)S(1)}, f32[128,768]{1,0:T(8,128)}, u32[]{:S(2)}) copy-start(f32[128,768]{1,0:T(8,128)} %get-tuple-element.94) | copy-start | bytes 1179652
  126.6 4.1 %copy-start.3 = (f32[1,768]{1,0:T(1,128)S(1)}, f32[1,768]{1,0:T(1,128)}, u32[]{:S(2)}) copy-start(f32[1,768]{1,0:T(1,128)} %get-tuple-element.128) | copy-start | bytes 9220
  130.6 0.7 copy-start.1
  153.0 2.1 copy-start.7
